TPU v7x, 256 devices: a whole 4x4x8 slice. The times are simulated.
256 devices in a mesh: elem: 32 (over y, z), mode: 8 (over x, core).
Axes of the slice: x: 4, y: 4, z: 8, core: 2. Of those that a mesh axis runs over, the one named last changes fastest.
Arguments:
- vel_x: float32 [81, 512, 1024], P(None, 'elem', 'mode'), may hold values from -6 to 6
- vel_y: float32 [81, 512, 1024], P(None, 'elem', 'mode'), may hold values from -6 to 6
- metrics: float32 [8, 81, 512], P(None, None, 'elem'), may hold values from -2 to 5, as said below
- slot_order: int32 [512], P('elem'), may hold values from 0 to 15, as said below
Outputs:
- new_vel_x: float32 [81, 512, 1024], P(None, 'elem', 'mode')
- new_vel_y: float32 [81, 512, 1024], P(None, 'elem', 'mode')
Inputs may be any that keep to these rules, and one draw needn't show every extreme that they name: `metrics`: rows 0 and 3 lie in 0.5 to 2 and rows 1 and 2 in -0.5 to 0.5; rows 4, 6 and 7 are positive, and |row 5| is at most 0.4 sqrt(row 4 row 6). `slot_order`: each aligned block of 16 entries, one sector's, is a permutation of 0 to 15.
All inputs are finite; a program needn't handle non-finite values.
Results may differ from a plain program's by a relative error of at most 0.0003.
Values sent between devices are 32-bit elements; how exact they have to be, the bound alone decides.
A program may use at most 128 MiB of HBM per device.

v0:
```python
import math

import jax
import jax.numpy as jnp
import numpy as np
from jax import lax
from jax.sharding import PartitionSpec as P

ORDER = 8
RAD = 4
MODES = 1024
PLANES = 1536
ITERS = 2


SIGMA = 2.0
WAVE = 64.0
HIGH = lax.Precision.HIGHEST


def padded_2(array, sides, width):
    for axis, dim in sides:
        size, length = (lax.axis_size(axis), array.shape[dim])
        up = [(i, (i + 1) % size) for i in range(size)]
        down = [(j, i) for i, j in up]
        last = lax.slice_in_dim(array, length - width, length, axis=dim)
        initial = lax.slice_in_dim(array, 0, width, axis=dim)
        before = lax.ppermute(last, axis, up)
        after = lax.ppermute(initial, axis, down)
        array = jnp.concatenate([before, array, after], axis=dim)
    return array


def legendre_value(order, point):
    previous = 1.0
    current = point
    for degree in range(2, order + 1):
        previous, current = (
            current,
            ((2 * degree - 1) * point * current - (degree - 1) * previous) / degree,
        )
    return (current, previous)


def gll_matrix(order):
    points = []
    for index in range(order + 1):
        point = -math.cos(math.pi * index / order)
        for sweep in range(100):
            high, lower = legendre_value(order, point)
            point = point - (point * high - lower) / ((order + 1) * high)
        points.append(point)
    points[0] = -1.0
    points[order] = 1.0
    values = [legendre_value(order, point)[0] for point in points]
    number = order + 1
    matrix = np.zeros((number, number))
    for row_index in range(number):
        for col_index in range(number):
            if row_index != col_index:
                matrix[row_index, col_index] = values[row_index] / (
                    values[col_index] * (points[row_index] - points[col_index])
                )
    matrix[0, 0] = -order * (order + 1) / 4.0
    matrix[order, order] = order * (order + 1) / 4.0
    return matrix


def basis_table(modes, planes):
    wave_index = jnp.arange(modes, dtype=jnp.int32)
    frequency = (wave_index + 1) // 2
    plane = jnp.arange(planes, dtype=jnp.int32)
    phase = frequency[:, None] * plane[None, :] % planes
    angle = 2.0 * math.pi / planes * phase.astype(jnp.float32)
    even = (wave_index % 2 == 0)[:, None]
    table = jnp.where(even, jnp.cos(angle), jnp.sin(angle))
    factor = jnp.where(wave_index == 0, math.sqrt(1.0 / planes), math.sqrt(2.0 / planes)).astype(
        jnp.float32
    )
    return table * factor[:, None]


def derivatives(field, dmatrix, geometry):
    along_i = jnp.einsum("pi,ijem->pjem", dmatrix, field, precision=HIGH)
    along_j = jnp.einsum("qj,ijem->iqem", dmatrix, field, precision=HIGH)
    grad_x = geometry[0][..., None] * along_i + geometry[1][..., None] * along_j
    grad_y = geometry[2][..., None] * along_i + geometry[3][..., None] * along_j
    return (grad_x, grad_y)


def wall_factors(points, radial):
    across = jnp.arange(points, dtype=jnp.int32)[:, None, None]
    along = jnp.arange(points, dtype=jnp.int32)[None, :, None]
    layer = jnp.arange(radial, dtype=jnp.int32)[None, None, :]
    wall = (layer == 0) & (across == 0) | (layer == radial - 1) & (across == points - 1)
    keep = jnp.where(wall, 0.0, 1.0).astype(jnp.float32)
    sides = jnp.where((along == 0) | (along == points - 1), 2.0, 1.0).astype(jnp.float32)
    inside = (across == 0) & (layer > 0) | (across == points - 1) & (layer < radial - 1)
    shared = jnp.where(inside, 2.0, 1.0).astype(jnp.float32)
    weight = keep / (sides * shared)
    return (keep, weight)


def helmholtz_local(field, geometry, shifts, dmatrix):
    along_i = jnp.einsum("pi,cijram->cpjram", dmatrix, field, precision=HIGH)
    along_j = jnp.einsum("qj,cijram->ciqram", dmatrix, field, precision=HIGH)
    g_aa = geometry[0][None, ..., None]
    g_ab = geometry[1][None, ..., None]
    g_bb = geometry[2][None, ..., None]
    jacob = geometry[3][None, ..., None]
    flux_i = g_aa * along_i + g_ab * along_j
    flux_j = g_ab * along_i + g_bb * along_j
    result = jnp.einsum("pi,cpjram->cijram", dmatrix, flux_i, precision=HIGH)
    result = result + jnp.einsum("qj,ciqram->cijram", dmatrix, flux_j, precision=HIGH)
    return result + shifts * jacob * field


def assemble_sector(field, keep):
    last = field.shape[1] - 1
    right = field[:, :, last]
    left = field[:, :, 0]
    rims = jnp.stack([left[:, :, :, 0], right[:, :, :, -1]], axis=3)
    padded = padded_2(rims, (("elem", 3),), 1)
    after = jnp.concatenate([left[:, :, :, 1:], padded[:, :, :, 3:4]], axis=3)
    shared = right + after
    before = padded[:, :, :, 0:1] + left[:, :, :, 0:1]
    new_left = jnp.concatenate([before, shared[:, :, :, :-1]], axis=3)
    field = field.at[:, :, last].set(shared).at[:, :, 0].set(new_left)
    outer = field[:, last, :, :-1]
    inner_side = field[:, 0, :, 1:]
    joined = outer + inner_side
    field = field.at[:, last, :, :-1].set(joined).at[:, 0, :, 1:].set(joined)
    return field * keep[None, :, :, :, None, None]


def inner(first, second, weight):
    return jnp.sum(first * second * weight[None, :, :, :, None, None], axis=(1, 2, 3, 4))


def expand(values):
    return values[:, None, None, None, None, :]


def body(vel_x, vel_y, metrics, slot_order):
    points = ORDER + 1
    nodes = points * points
    local_elems = vel_x.shape[1]
    local_modes = vel_x.shape[2]
    groups = lax.axis_size("mode")
    share = local_elems // groups
    columns = local_elems // RAD
    dmatrix = jnp.asarray(gll_matrix(ORDER), jnp.float32)
    table = basis_table(MODES, PLANES)
    geo = metrics.reshape(8, points, points, local_elems)
    shaped_x = vel_x.reshape(points, points, local_elems, local_modes)
    shaped_y = vel_y.reshape(points, points, local_elems, local_modes)
    xx_dx, xx_dy = derivatives(shaped_x, dmatrix, geo)
    yy_dx, yy_dy = derivatives(shaped_y, dmatrix, geo)
    stacked = jnp.stack([shaped_x, shaped_y, xx_dx, xx_dy, yy_dx, yy_dy]).reshape(
        6, nodes, local_elems, local_modes
    )
    arrived = lax.all_to_all(stacked, "mode", split_axis=2, concat_axis=3, tiled=True)
    planes = jnp.dot(arrived.reshape(-1, MODES), table, precision=HIGH).reshape(
        6, points, points, share, PLANES
    )
    phys_x, phys_y = (planes[0], planes[1])
    xx_dx, xx_dy, yy_dx, yy_dy = (planes[2], planes[3], planes[4], planes[5])
    first = phys_x * xx_dx + phys_y * xx_dy
    second = phys_x * yy_dx + phys_y * yy_dy
    products = jnp.stack([first, second]).reshape(-1, PLANES)
    spectral = jnp.dot(products, table.T, precision=HIGH).reshape(2, nodes, share, MODES)
    nonlin = lax.all_to_all(spectral, "mode", split_axis=3, concat_axis=2, tiled=True)
    velocity = jnp.stack([vel_x, vel_y])
    source = metrics[7][None, :, :, None] * (SIGMA * velocity - nonlin)
    selector = (slot_order[:, None] == jnp.arange(local_elems, dtype=jnp.int32)[None, :]).astype(
        jnp.float32
    )
    grid_src = jnp.einsum("ps,cnsm->cnpm", selector, source, precision=HIGH).reshape(
        2, points, points, RAD, columns, local_modes
    )
    geometry = jnp.einsum("ps,gns->gnp", selector, metrics[4:8], precision=HIGH).reshape(
        4, points, points, RAD, columns
    )
    keep, weight = wall_factors(points, RAD)
    global_mode = lax.axis_index("mode") * local_modes + jnp.arange(local_modes, dtype=jnp.int32)
    frequency = ((global_mode + 1) // 2).astype(jnp.float32)
    shifts = SIGMA + (frequency / WAVE) ** 2
    rhs = assemble_sector(grid_src, keep)
    solution = jnp.zeros_like(rhs)
    residual = rhs

    def squares(vector):
        return lax.psum(inner(vector, vector, weight), "elem")

    direction = rhs
    norm_now = squares(residual)
    for step in range(ITERS):
        image = assemble_sector(helmholtz_local(direction, geometry, shifts, dmatrix), keep)
        alpha = norm_now / lax.psum(inner(direction, image, weight), "elem")
        solution = solution + expand(alpha) * direction
        residual = residual - expand(alpha) * image
        if step + 1 < ITERS:
            norm_next = squares(residual)
            direction = residual + expand(norm_next / norm_now) * direction
            norm_now = norm_next
    flat = solution.reshape(2, nodes, local_elems, local_modes)
    stored = jnp.einsum("ps,cnpm->cnsm", selector, flat, precision=HIGH)
    return (stored[0], stored[1])


def solution(mesh):
    placed = (P(None, "elem", "mode"), P(None, "elem", "mode"), P(None, None, "elem"), P("elem"))
    return jax.shard_map(
        body,
        mesh=mesh,
        in_specs=placed,
        out_specs=(P(None, "elem", "mode"), P(None, "elem", "mode")),
        check_vma=False,
    )
```

profile of v0, /device:TPU:2, one launch (start us, length us, event | category | flops | bytes accessed | tf_op | source)
XLA Modules:
  0.0 532.8 jit_solution(16473721723896540623)
XLA Ops:
  7.8 3.1 fusion.55
  12.1 3.4 copy.131
  15.4 6.9 %all-to-all-start = ((f32[6,81,16,128]{3,1,0,2:T(8,128)}), f32[6,81,16,128]{3,1,0,2:T(8,128)}, u32[]{:S(2)}, u32[]{:S(2)}) async-start(f32[6,81,16,128]{3,1,0,2:T(8,128)} %copy.131), calls=%async_computation | async-start | bytes 8650752 | tf_op jit(solution)/shard_map/all_to_all | solution.py:162
  23.8 28.6 %select_multiply_fusion.5 = f32[1024,1536]{1,0:T(8,128)} fusion(f32[1024]{0:T(1024)S(1)} %fusion.94, s32[1024]{0:T(1024)S(1)} %add_select_fusion.1, pred[1024]{0:T(1024)(128)(4,1)S(1)} %fusion.84), kind=kLoop, calls=%fused_computation.5.clone.1.clone.1 | loop fusion | flops 17301504 | bytes 6300672 | tf_op jit(solution)/shard_map/dot_general | solution.py:163
  52.4 19.6 %all-to-all-done = f32[6,81,16,128]{3,1,0,2:T(8,128)} async-done(((f32[6,81,16,128]{3,1,0,2:T(8,128)}), f32[6,81,16,128]{3,1,0,2:T(8,128)}, u32[]{:S(2)}, u32[]{:S(2)}) %all-to-all-start) | async-done | bytes 3981344 | tf_op jit(solution)/shard_map/all_to_all | solution.py:162
  72.0 4.5 copy.132
  79.5 19.4 %fusion.7 = f32[972,1536]{1,0:T(8,128)S(1)} fusion(f32[972,1024]{1,0:T(8,128)S(1)} %bitcast.238, f32[1024,1536]{1,0:T(8,128)S(1)} %bitcast.234), kind=kOutput, calls=%fused_computation.10 | convolution fusion | flops 18345885696 | bytes 16244736 | tf_op jit(solution)/shard_map/dot_general | solution.py:163
  105.7 34.9 %fusion.2 = f32[2,81,2,1024]{3,1,2,0:T(8,128)S(1)} fusion(f32[1024]{0:T(1024)S(1)} %fusion.94, s32[1024]{0:T(1024)S(1)} %add_select_fusion.1, pred[1024]{0:T(1024)(128)(4,1)S(1)} %fusion.84, f32[2,81,2,1536]{3,1,2,0:T(8,128)S(1)} %fusion.132), kind=kOutput, calls=%fused_computation.3 | convolution fusion | flops 6132596736 | bytes 3326976 | tf_op jit(solution)/shard_map/dot_general | solution.py:171
  142.9 5.8 %all-to-all-start.1 = ((f32[2,81,2,1024]{1,2,0,3:T(2,128)}), f32[2,81,2,1024]{1,2,0,3:T(2,128)}, u32[]{:S(2)}, u32[]{:S(2)}) async-start(f32[2,81,2,1024]{1,2,0,3:T(2,128)} %copy.135), calls=%async_computation.1 | async-start | bytes 4194304 | tf_op jit(solution)/shard_map/all_to_all | solution.py:172
  151.5 23.1 %all-to-all-done.1 = f32[2,81,2,1024]{1,2,0,3:T(2,128)} async-done(((f32[2,81,2,1024]{1,2,0,3:T(2,128)}), f32[2,81,2,1024]{1,2,0,3:T(2,128)}, u32[]{:S(2)}, u32[]{:S(2)}) %all-to-all-start.1) | async-done | bytes 1327136 | tf_op jit(solution)/shard_map/all_to_all | solution.py:172
  185.4 5.4 %collective-permute-done.1 = f32[2,9,4,1,128]{4,1,3,2,0:T(8,128)} collective-permute-done((f32[2,9,4,1,128]{4,1,3,2,0:T(8,128)S(1)}, f32[2,9,4,1,128]{4,1,3,2,0:T(8,128)}, u32[]{:S(2)}, u32[]{:S(2)}) %collective-permute-start.1) | collective-permute-done | bytes 36896 | tf_op jit(solution)/shard_map/ppermute | solution.py:28
  198.3 4.0 scatter.44
  202.3 3.5 broadcast_select_fusion.2
  205.8 4.3 scatter.45
  213.9 3.8 fusion.27
  220.8 5.6 %fusion.23 = f32[2,9,9,4,4,128]{5,1,4,3,2,0:T(8,128)S(1)} fusion(f32[2,9,4,4,128,9]{4,5,3,2,1,0:T(8,128)S(1)} %fusion.34, f32[9,9,1,1,1,1]{1,0,5,4,3,2:T(8,128)S(1)} %copy-done.15, f32[2,9,4,4,128,9]{4,5,3,2,1,0:T(8,128)S(1)} %get-tuple-element.191, f32[2,9,4,4,128,9]{4,5,3,2,1,0:T(8,128)S(1)} %fusion.36, f32[9,9,4,4]{0,3,2,1:T(4,128)S(1)} %copy-done.9, ...), kind=kOutput, calls=%fused_computation.32 | convolution fusion | flops 38154240 | bytes 7309908 | tf_op jit(solution)/shard_map/pi,cpjram->cijram/dot_general | solution.py:113
  227.3 6.9 %collective-permute-done.3 = f32[2,9,4,1,128]{4,1,3,2,0:T(8,128)S(1)} collective-permute-done((f32[2,9,4,1,128]{4,1,3,2,0:T(8,128)S(1)}, f32[2,9,4,1,128]{4,1,3,2,0:T(8,128)S(1)}, u32[]{:S(2)}, u32[]{:S(2)}) %collective-permute-start.3) | collective-permute-done | bytes 36896 | tf_op jit(solution)/shard_map/ppermute | solution.py:28
  241.6 4.8 scatter.50
  246.3 3.9 broadcast_select_fusion.1
  250.2 5.3 scatter.51
  255.5 3.1 multiply_reduce_fusion.2
  258.6 75.6 %all-reduce = (f32[2,128]{1,0:T(2,128)}, f32[2,128]{1,0:T(2,128)}) all-reduce(f32[2,128]{1,0:T(2,128)} %get-tuple-element.147, f32[2,128]{1,0:T(2,128)} %get-tuple-element.146), channel_id=1, replica_groups=mesh['elem'=32,'mode'=8] {'elem'}, use_global_device_ids=true, to_apply=%region_2.3 | all-reduce | flops 512 | bytes 4096 | tf_op jit(solution)/shard_map/psum | solution.py:193
  338.5 70.3 %psum.30 = f32[2,128]{1,0:T(2,128)} all-reduce(f32[2,128]{1,0:T(2,128)} %multiply_reduce_fusion.1), channel_id=1, replica_groups=mesh['elem'=32,'mode'=8] {'elem'}, use_global_device_ids=true, to_apply=%region_6.7 | all-reduce | flops 256 | bytes 2048 | tf_op jit(solution)/shard_map/psum | solution.py:193
  411.8 3.1 fusion.32
  415.0 4.1 fusion.21
  419.1 3.1 fusion.28
  422.2 3.2 fusion.20
  432.5 5.2 collective-permute-done.5
  440.1 4.6 scatter.56
  444.7 3.3 broadcast_select_fusion
  448.0 5.2 scatter.59
  456.2 71.6 %psum.31 = f32[2,128]{1,0:T(2,128)S(1)} all-reduce(f32[2,128]{1,0:T(2,128)S(1)} %multiply_reduce_fusion), channel_id=1, replica_groups=mesh['elem'=32,'mode'=8] {'elem'}, use_global_device_ids=true, to_apply=%region_8.9 | all-reduce | flops 256 | bytes 2048 | tf_op jit(solution)/shard_map/psum | solution.py:199
  (180 shorter events, 81.9 us)
Async XLA Ops:
  0.6 2.4 copy-start.18
  0.6 2.4 copy-start.1
  0.7 4.7 copy-start.19
  3.1 3.4 copy-start.2
  15.4 8.2 %copy-start.25 = (s32[16]{0:T(128)S(1)}, s32[16]{0:T(128)}, u32[]{:S(2)}) copy-start(s32[16]{0:T(128)} %param.32) | copy-start | bytes 196
  15.4 56.6 %all-to-all-start = ((f32[6,81,16,128]{3,1,0,2:T(8,128)}), f32[6,81,16,128]{3,1,0,2:T(8,128)}, u32[]{:S(2)}, u32[]{:S(2)}) async-start(f32[6,81,16,128]{3,1,0,2:T(8,128)} %copy.131), calls=%async_computation | async-start | bytes 8650752 | tf_op jit(solution)/shard_map/all_to_all | solution.py:162
  76.8 2.6 slice-start.1
  142.9 6.9 %copy-start.29 = (s32[6]{0:T(128)S(1)}, s32[6]{0:T(128)}, u32[]{:S(2)}) copy-start(s32[6]{0:T(128)} %constant.348.clone.1) | copy-start | bytes 76
  142.9 31.7 %all-to-all-start.1 = ((f32[2,81,2,1024]{1,2,0,3:T(2,128)}), f32[2,81,2,1024]{1,2,0,3:T(2,128)}, u32[]{:S(2)}, u32[]{:S(2)}) async-start(f32[2,81,2,1024]{1,2,0,3:T(2,128)} %copy.135), calls=%async_computation.1 | async-start | bytes 4194304 | tf_op jit(solution)/shard_map/all_to_all | solution.py:172
  174.6 4.9 copy-start.17
  174.6 4.9 copy-start.26
  181.7 12.1 %copy-start.7 = (f32[2,81,128,16]{2,3,1,0:T(8,128)S(1)}, f32[2,81,128,16]{2,3,1,0:T(8,128)}, u32[]{:S(2)}) copy-start(f32[2,81,128,16]{2,3,1,0:T(8,128)} %copy-done.6) | copy-start | bytes 3981316
  181.8 9.0 %collective-permute-start.1 = (f32[2,9,4,1,128]{4,1,3,2,0:T(8,128)S(1)}, f32[2,9,4,1,128]{4,1,3,2,0:T(8,128)}, u32[]{:S(2)}, u32[]{:S(2)}) collective-permute-start(f32[2,9,4,1,128]{4,1,3,2,0:T(8,128)S(1)} %slice.655), channel_id=1, source_target_pairs={{0,8},{8,16},{16,24},{24,32},{32,40},{40,48},{48,56},{56,64},{64,7... | collective-permute-start | bytes 110600 | tf_op jit(solution)/shard_map/ppermute | solution.py:28
  191.6 4.3 collective-permute-start
  210.8 3.1 copy-start.9
  210.8 3.1 copy-start.13
  217.7 3.1 copy-start.11
  220.8 5.8 %copy-start.24 = (f32[9,4]{0,1:T(4,128)S(1)}, f32[9,4]{0,1:T(4,128)}, u32[]{:S(2)}) copy-start(f32[9,4]{0,1:T(4,128)} %get-tuple-element.188) | copy-start | bytes 436
  220.8 5.8 %copy-start.28 = (f32[9]{0:T(128)S(1)}, f32[9]{0:T(128)}, u32[]{:S(2)}) copy-start(f32[9]{0:T(128)} %or_select_fusion.1) | copy-start | bytes 112
  226.5 7.7 %collective-permute-start.3 = (f32[2,9,4,1,128]{4,1,3,2,0:T(8,128)S(1)}, f32[2,9,4,1,128]{4,1,3,2,0:T(8,128)S(1)}, u32[]{:S(2)}, u32[]{:S(2)}) collective-permute-start(f32[2,9,4,1,128]{4,1,3,2,0:T(8,128)S(1)} %slice.667), channel_id=1, source_target_pairs={{0,8},{8,16},{16,24},{24,32},{32,40},{40,48},{48,56},{56,64},{64,7... | collective-permute-start | bytes 110600 | tf_op jit(solution)/shard_map/ppermute | solution.py:28
  234.2 4.3 collective-permute-start.2
  411.8 10.4 %copy-start = (f32[2,9,9,4,4,128]{5,1,4,3,2,0:T(8,128)}, f32[2,9,9,4,4,128]{5,1,4,3,2,0:T(8,128)S(1)}, u32[]{:S(2)}) copy-start(f32[2,9,9,4,4,128]{5,1,4,3,2,0:T(8,128)S(1)} %multiply_add_fusion.1) | copy-start | bytes 3981316
  411.8 3.1 copy-start.10
  411.8 3.1 copy-start.12
  411.8 3.1 copy-start.14
  419.1 3.1 copy-start.23
  425.5 4.3 collective-permute-start.4
  429.9 7.9 %collective-permute-start.5 = (f32[2,9,4,1,128]{4,1,3,2,0:T(8,128)S(1)}, f32[2,9,4,1,128]{4,1,3,2,0:T(8,128)S(1)}, u32[]{:S(2)}, u32[]{:S(2)}) collective-permute-start(f32[2,9,4,1,128]{4,1,3,2,0:T(8,128)S(1)} %slice.675), channel_id=1, source_target_pairs={{0,8},{8,16},{16,24},{24,32},{32,40},{40,48},{48,56},{56,64},{64,7... | collective-permute-start | bytes 110600 | tf_op jit(solution)/shard_map/ppermute | solution.py:28
  437.8 2.2 copy-start.5
  437.8 15.4 %copy-start.16 = (f32[9,9,4]{0,2,1:T(4,128)S(1)}, f32[9,9,4]{0,2,1:T(4,128)}, u32[]{:S(2)}) copy-start(f32[9,9,4]{0,2,1:T(4,128)} %multiply_divide_fusion) | copy-start | bytes 3892
  453.2 74.6 %copy-start.22 = (f32[2,128]{1,0:T(2,128)S(1)}, f32[2,128]{1,0:T(2,128)}, u32[]{:S(2)}) copy-start(f32[2,128]{1,0:T(2,128)} %psum.30) | copy-start | bytes 3076
  453.2 74.6 %copy-start.21 = (f32[2,128]{1,0:T(2,128)S(1)}, f32[2,128]{1,0:T(2,128)}, u32[]{:S(2)}) copy-start(f32[2,128]{1,0:T(2,128)} %copy-done.20) | copy-start | bytes 3076
  (8 other events, 9.5 us)
where the time goes:
time: 541 us; the launch traced here: 533 us
  blocking collectives  218 us (40%)
  matrix products  94.2 us (17%)
  local copies, waits for them, and re-layouts  70.1 us (13%)
  waiting for transfers between devices  66.3 us (12%)
  other arithmetic  61.2 us (11%)
  starting transfers between devices  21.6 us (4%)
    psum x2, blocking collectives, squares(): return lax.psum(inner(vector, vector, weight), 'elem')  146 us
    psum x1, blocking collectives, body(): alpha = norm_now / lax.psum(inner(direction, image, weight), 'elem')  71.6 us
    dot_general x1, matrix products, body(): jnp.dot(products, table.T, precision=HIGH).reshape(2, nodes, share, MODES)  34.9 us
    dot_general x1, other arithmetic, body(): jnp.dot(arrived.reshape(-1, MODES), table, precision=HIGH)  28.6 us
    scatter x6, local copies, waits for them, and re-layouts, assemble_sector(): field = field.at[:, last, :, :-1].set(joined).at[:, 0, :, 1:].set(joined)  28.1 us
    all_to_all x1, waiting for transfers between devices, body(): lax.all_to_all(spectral, 'mode', split_axis=3, concat_axis=2, tiled=True)  23.1 us
    all_to_all x1, waiting for transfers between devices, body(): lax.all_to_all(stacked, 'mode', split_axis=2, concat_axis=3, tiled=True)  19.6 us
    dot_general x1, matrix products, body(): jnp.dot(arrived.reshape(-1, MODES), table, precision=HIGH)  19.4 us
  transfers between devices with their start and end apart: 8, of which 8 were waited for; matrix products, arithmetic and copies ran while one was open for 7% of the time, Pallas kernels for 0%

commit v1 on v0

v1 whole, which is shorter than its diff:
```python
import functools
import math

import jax
import jax.numpy as jnp
import ml_dtypes
import numpy as np
from jax import lax
from jax.experimental import pallas as pl
from jax.experimental.pallas import tpu as pltpu
from jax.sharding import PartitionSpec as P

ORDER = 8
NP = ORDER + 1
NODES = NP * NP
ROWS = 88
KROWS = 96
EDGE = NODES - NP
RAD = 4
AZ = 4
ELEMS = 16
MODES = 1024
PLANES = 1536
LANES = 128
CHUNK = 256
GROUPS = 8
ZRING = 8
SIGMA = 2.0
WAVE = 64.0
MESH = pl.DeviceIdType.MESH
F32 = jnp.float32
BF16 = jnp.bfloat16


def legendre_value(order, point):
    previous = 1.0
    current = point
    for degree in range(2, order + 1):
        previous, current = (
            current,
            ((2 * degree - 1) * point * current - (degree - 1) * previous) / degree,
        )
    return (current, previous)


def gll_matrix(order):
    points = []
    for index in range(order + 1):
        point = -math.cos(math.pi * index / order)
        for sweep in range(100):
            high, lower = legendre_value(order, point)
            point = point - (point * high - lower) / ((order + 1) * high)
        points.append(point)
    points[0] = -1.0
    points[order] = 1.0
    values = [legendre_value(order, point)[0] for point in points]
    number = order + 1
    matrix = np.zeros((number, number))
    for row_index in range(number):
        for col_index in range(number):
            if row_index != col_index:
                matrix[row_index, col_index] = values[row_index] / (
                    values[col_index] * (points[row_index] - points[col_index])
                )
    matrix[0, 0] = -order * (order + 1) / 4.0
    matrix[order, order] = order * (order + 1) / 4.0
    return matrix


def halves(array):
    array = np.asarray(array, np.float32)
    high = array.astype(ml_dtypes.bfloat16)
    low = (array - high.astype(np.float32)).astype(ml_dtypes.bfloat16)
    return high, low


@functools.lru_cache(maxsize=None)
def constants():
    wave = np.arange(MODES)
    freq = (wave + 1) // 2
    phase = freq[:, None] * np.arange(PLANES)[None, :] % PLANES
    angle = 2.0 * np.pi / PLANES * phase
    table = np.where((wave % 2 == 0)[:, None], np.cos(angle), np.sin(angle))
    table = table * np.where(wave == 0, math.sqrt(1.0 / PLANES), math.sqrt(2.0 / PLANES))[:, None]
    high, low = halves(table)
    there = np.stack([high, low]).reshape(2, MODES, PLANES // CHUNK, CHUNK).transpose(0, 2, 1, 3)
    back = np.stack([high.T, low.T]).reshape(2, PLANES, MODES // CHUNK, CHUNK).transpose(0, 2, 1, 3)
    dmat = gll_matrix(ORDER).astype(np.float32)
    eye = np.eye(NP, dtype=np.float32)
    grad = np.zeros((2, ROWS, ROWS), np.float32)
    grad[0, :NODES, :NODES] = np.kron(dmat, eye)
    grad[1, :NODES, :NODES] = np.kron(eye, dmat)
    ghigh, glow = halves(grad.reshape(2 * ROWS, ROWS))
    gmat = np.zeros((4 * ROWS, 2 * KROWS), ml_dtypes.bfloat16)
    gmat[: 2 * ROWS, :ROWS] = ghigh
    gmat[: 2 * ROWS, KROWS : KROWS + ROWS] = ghigh
    gmat[2 * ROWS :, :ROWS] = glow
    dhigh, dlow = halves(grad.transpose(2, 0, 1).reshape(ROWS, 2 * ROWS))
    dmat2 = np.zeros((2 * KROWS, 2 * ROWS), ml_dtypes.bfloat16)
    dmat2[:ROWS] = dhigh
    dmat2[KROWS : KROWS + ROWS] = dlow
    return np.ascontiguousarray(there), np.ascontiguousarray(back), gmat, dmat2


def split(value):
    high = value.astype(BF16)
    return high, (value - high.astype(F32)).astype(BF16)


def split_rows(value):
    high = value.astype(BF16).astype(F32)
    gap = jnp.zeros((KROWS - ROWS, value.shape[1]), F32)
    return jnp.concatenate([high, gap, value - high, gap], axis=0).astype(BF16)


def mm(a, b):
    return jnp.dot(a, b, preferred_element_type=F32)


def fold(value):
    total = jnp.sum(value.reshape(ROWS // 8, 8, value.shape[1]), axis=0)
    out = total[:, :LANES]
    for at in range(1, value.shape[1] // LANES):
        out = out + total[:, at * LANES : (at + 1) * LANES]
    return out


def position(rank, second):
    return ((rank % 2) * 2 + second) * AZ + rank // 2


def kernel(
    size_e,
    velx_hbm,
    vely_hbm,
    met_hbm,
    slots,
    there_hbm,
    back_hbm,
    gmat_hbm,
    dmat_hbm,
    out,
    vel,
    met,
    there,
    back,
    gmat,
    dmat,
    snd,
    rv,
    act,
    wave,
    edge,
    pgeo,
    geo,
    wts,
    ret,
    rv2,
    bf,
    yf,
    hs,
    hr,
    acc,
    part,
    gat_z,
    gat_y,
    in_sem,
    s1,
    r1,
    own,
    s2,
    r2,
    hsem,
    hrem,
    as_z,
    ar_z,
    as_y,
    ar_y,
):
    me_e = lax.axis_index("elem")
    me = lax.axis_index("mode")
    chip, core = me // 2, me % 2
    zed, why = me_e % ZRING, me_e // ZRING
    size_y = size_e // ZRING
    left = (me_e + size_e - 1) % size_e
    right = (me_e + 1) % size_e
    peers = [
        (((chip + dc) % 4) * 2 + (core + cc) % 2)
        for dc, cc in ((2, 0), (2, 1), (1, 0), (3, 0), (1, 1), (3, 1), (0, 1))
    ]
    z_peers = [why * ZRING + (zed + k) % ZRING for k in range(1, ZRING)]
    y_peers = [((why + k) % size_y) * ZRING + zed for k in range(1, size_y)]

    loads = [
        pltpu.make_async_copy(velx_hbm, vel.at[0], in_sem.at[0]),
        pltpu.make_async_copy(vely_hbm, vel.at[1], in_sem.at[1]),
        pltpu.make_async_copy(met_hbm, met, in_sem.at[2]),
        pltpu.make_async_copy(gmat_hbm, gmat, in_sem.at[3]),
        pltpu.make_async_copy(dmat_hbm, dmat, in_sem.at[4]),
        pltpu.make_async_copy(there_hbm, there, in_sem.at[5]),
        pltpu.make_async_copy(back_hbm, back, in_sem.at[6]),
    ]
    for copy in loads:
        copy.start()

    tail = jnp.zeros((2, 8, LANES), F32)
    for p in range(ELEMS):
        snd[p, :, ROWS - 8 :, :] = tail
        rv[p // 2, p % 2, :, ROWS - 8 :, :] = tail
        rv2[p, :, EDGE : EDGE + 8, :] = tail
        rv2[p, :, EDGE + 8 :, :] = tail

    barrier = pltpu.get_barrier_semaphore()
    for peer in peers:
        pl.semaphore_signal(barrier, inc=1, device_id=(me_e, peer), device_id_type=MESH)
    for peer in z_peers + y_peers + [left, right]:
        pl.semaphore_signal(barrier, inc=1, device_id=(peer, me), device_id_type=MESH)

    pl.semaphore_wait(barrier, len(peers) + len(z_peers) + len(y_peers) + 2)

    loads[0].wait()
    loads[1].wait()

    def gather(p):
        slot = slots[p]
        for c in range(2):
            snd[p, c, 0:NODES, :] = vel[c, pl.ds(slot, NODES, stride=ELEMS), :]

    sends = []
    arrivals = [[], []]
    locals_ = []
    for e in range(2):
        for k, peer in enumerate(peers):
            p = position(peer, e)
            gather(p)
            copy = pltpu.make_async_remote_copy(
                src_ref=snd.at[p, :, pl.ds(0, NODES)],
                dst_ref=rv.at[me, e, :, pl.ds(0, NODES)],
                send_sem=s1.at[e, k],
                recv_sem=r1.at[e, me],
                device_id=(me_e, peer),
                device_id_type=MESH,
            )
            copy.start()
            sends.append(copy)
        p = position(me, e)
        gather(p)
        copy = pltpu.make_async_copy(
            snd.at[p, :, pl.ds(0, NODES)], rv.at[me, e, :, pl.ds(0, NODES)], own.at[e]
        )
        copy.start()
        locals_.append(copy)
        for k, peer in enumerate(peers):
            arrivals[e].append(
                pltpu.make_async_remote_copy(
                    src_ref=snd.at[0, :, pl.ds(0, NODES)],
                    dst_ref=rv.at[peer, e, :, pl.ds(0, NODES)],
                    send_sem=s1.at[e, k],
                    recv_sem=r1.at[e, peer],
                    device_id=(me_e, peer),
                    device_id_type=MESH,
                )
            )

    loads[2].wait()
    loads[3].wait()
    loads[4].wait()
    row16 = lax.broadcasted_iota(jnp.int32, (ELEMS, LANES), 0)

    def picker(p):
        return jnp.where(row16 == slots[p], 1.0, 0.0).astype(BF16)

    def spread(factors, pick):
        gap = jnp.zeros((ROWS - NODES, ELEMS), F32)
        full = jnp.concatenate([factors, gap], axis=0)
        high = full.astype(BF16)
        rest = full - high.astype(F32)
        mid = rest.astype(BF16)
        low = (rest - mid.astype(F32)).astype(BF16)
        return mm(high, pick) + mm(mid, pick) + mm(low, pick)

    mine = jnp.concatenate([picker(position(me, 0)), picker(position(me, 1))], axis=1)
    jac = spread(met[7], mine)
    for g in range(4):
        full = spread(met[g], mine) * jac
        pgeo[0, g] = full[:, :LANES]
        pgeo[1, g] = full[:, LANES:]

    def spread_row(r, carry):
        pick = jnp.concatenate([picker(r * AZ + a) for a in range(AZ)], axis=1)
        for g in range(4):
            full = spread(met[4 + g], pick)
            for a in range(AZ):
                geo[g, r * AZ + a] = full[:, a * LANES : (a + 1) * LANES]
        return carry

    lax.fori_loop(0, RAD, spread_row, 0)

    node = lax.broadcasted_iota(jnp.int32, (ROWS, LANES), 0)
    along = node % NP
    sides = jnp.where((along == 0) | (along == NP - 1), 0.5, 1.0).astype(F32)
    sides = jnp.where(node < NODES, sides, 0.0)
    first, last = node < NP, node >= EDGE
    wts[0] = jnp.where(first, 0.0, jnp.where(last, 0.5, 1.0)) * sides
    wts[1] = jnp.where(first | last, 0.5, 1.0) * sides
    wts[2] = wts[1]
    wts[3] = jnp.where(last, 0.0, jnp.where(first, 0.5, 1.0)) * sides

    lane = lax.broadcasted_iota(jnp.int32, (1, LANES), 1) + me * LANES
    freq = ((lane + 1) // 2).astype(F32) / WAVE
    lam = SIGMA + freq * freq

    acc[...] = jnp.zeros_like(acc)

    ret_sends = []
    ret_locals = []
    for e in range(2):
        for copy in arrivals[e]:
            copy.wait_recv()
        locals_[e].wait()
        for src in range(GROUPS):
            both = rv[src, e].reshape(2 * ROWS, LANES)
            high, low = split(both)
            act[0 : 2 * ROWS, src * LANES : (src + 1) * LANES] = high
            act[2 * ROWS :, src * LANES : (src + 1) * LANES] = low
        if e == 0:
            loads[5].wait()

        def planes(z, carry, e=e):
            top = mm(act[...], there[0, z])
            field = top[: 2 * ROWS] + top[2 * ROWS :] + mm(act[0 : 2 * ROWS, :], there[1, z])
            u, v = field[:ROWS], field[ROWS:]
            diff = mm(gmat[...], split_rows(jnp.concatenate([u, v], axis=1)))
            diff = diff[: 2 * ROWS] + diff[2 * ROWS :]
            m = [jnp.concatenate([pgeo[e, g]] * (CHUNK // LANES), axis=1) for g in range(4)]
            by_i = u * m[0] + v * m[2]
            by_j = u * m[1] + v * m[3]
            for c in range(2):
                cols = slice(c * CHUNK, (c + 1) * CHUNK)
                prod = by_i * diff[:ROWS, cols] + by_j * diff[ROWS:, cols]
                if e == 0:
                    edge[c, z] = prod[EDGE:]
                else:
                    lower = prod[:16] + edge[c, z]
                    prod = jnp.concatenate([lower, prod[16:]], axis=0)
                if c == 0:
                    keep = prod
            high, low = split(jnp.concatenate([keep, prod], axis=0))
            at = pl.ds(pl.multiple_of(z * CHUNK, CHUNK), CHUNK)
            wave[0 : 2 * ROWS, at] = high
            wave[2 * ROWS :, at] = low
            return carry

        lax.fori_loop(0, PLANES // CHUNK, planes, 0)
        if e == 0:
            loads[6].wait()

        count = EDGE if e == 0 else NODES
        for step, dc in enumerate((2, 1, 3, 0)):
            n = (chip + dc) % 4
            top = mm(wave[...], back[0, n])
            hat = top[: 2 * ROWS] + top[2 * ROWS :] + mm(wave[0 : 2 * ROWS, :], back[1, n])
            for cc in range(2):
                pass
            for half in range(2):
                ret[e, n * 2 + half] = hat[:, half * LANES : (half + 1) * LANES].reshape(2, ROWS, LANES)
            for cc in range(2):
                peer = n * 2 + (core + cc) % 2
                src = ret.at[e, peer, :, pl.ds(0, count)]
                dst = rv2.at[position(me, e), :, pl.ds(0, count)]
                if dc == 0 and cc == 0:
                    copy = pltpu.make_async_copy(src, dst, own.at[2 + e])
                    ret_locals.append(copy)
                else:
                    copy = pltpu.make_async_remote_copy(
                        src_ref=src,
                        dst_ref=dst,
                        send_sem=s2.at[e, step * 2 + cc],
                        recv_sem=r2.at[e, me],
                        device_id=(me_e, peer),
                        device_id_type=MESH,
                    )
                    ret_sends.append(copy)
                copy.start()

    ret_arrivals = []
    for e in range(2):
        count = EDGE if e == 0 else NODES
        for peer in peers:
            ret_arrivals.append(
                pltpu.make_async_remote_copy(
                    src_ref=ret.at[e, 0, :, pl.ds(0, count)],
                    dst_ref=rv2.at[position(peer, e), :, pl.ds(0, count)],
                    send_sem=s2.at[e, 0],
                    recv_sem=r2.at[e, peer],
                    device_id=(me_e, peer),
                    device_id_type=MESH,
                )
            )
    for copy in ret_arrivals:
        copy.wait_recv()
    for copy in ret_locals:
        copy.wait()

    halo_sends = []

    def assemble_start(field, c, which):
        def column(a, carry):
            for r in range(RAD - 1):
                up, down = r * AZ + a, (r + 1) * AZ + a
                joined = field[c, up, EDGE : EDGE + 8] + field[c, down, 0:8]
                corner = field[c, up, EDGE + 8 : NODES] + field[c, down, 8:NP]
                field[c, up, EDGE : EDGE + 8] = joined
                field[c, down, 0:8] = joined
                field[c, up, EDGE + 8 : NODES] = corner
                field[c, down, 8:NP] = corner
            field[c, a, 0:8] = jnp.zeros((8, LANES), F32)
            field[c, a, 8:NP] = jnp.zeros((1, LANES), F32)
            end = (RAD - 1) * AZ + a
            field[c, end, EDGE : EDGE + 8] = jnp.zeros((8, LANES), F32)
            field[c, end, EDGE + 8 : NODES] = jnp.zeros((1, LANES), F32)
            return carry

        lax.fori_loop(0, AZ, column, 0)
        for r in range(RAD):
            hs[which, c, 0, r, 0:NP] = field[c, r * AZ, pl.ds(0, NP, stride=NP), :]
            hs[which, c, 1, r, 0:NP] = field[c, r * AZ + AZ - 1, pl.ds(NP - 1, NP, stride=NP), :]
        copies = []
        for side, peer in ((0, left), (1, right)):
            copy = pltpu.make_async_remote_copy(
                src_ref=hs.at[which, c, side, :, pl.ds(0, NP)],
                dst_ref=hr.at[which, c, side, :, pl.ds(0, NP)],
                send_sem=hsem.at[which, c, side],
                recv_sem=hrem.at[which, c, side],
                device_id=(peer, me),
                device_id_type=MESH,
            )
            copy.start()
            copies.append(copy)
        halo_sends.extend(copies)

        def joints(r, carry):
            for a in range(AZ - 1):
                p = r * AZ + a
                shared = (
                    field[c, p, pl.ds(NP - 1, NP, stride=NP), :]
                    + field[c, p + 1, pl.ds(0, NP, stride=NP), :]
                )
                field[c, p, pl.ds(NP - 1, NP, stride=NP), :] = shared
                field[c, p + 1, pl.ds(0, NP, stride=NP), :] = shared
            return carry

        lax.fori_loop(0, RAD, joints, 0)
        return copies

    def assemble_finish(field, c, which, copies):
        for copy in copies:
            copy.wait_recv()
        for r in range(RAD):
            p = r * AZ + AZ - 1
            at = pl.ds(NP - 1, NP, stride=NP)
            field[c, p, at, :] = field[c, p, at, :] + hr[which, c, 0, r, 0:NP]
            p = r * AZ
            at = pl.ds(0, NP, stride=NP)
            field[c, p, at, :] = field[c, p, at, :] + hr[which, c, 1, r, 0:NP]

    def pair(ref, c, p0, p1):
        return jnp.concatenate([ref[c, p0], ref[c, p1]], axis=1)

    def fluxes(x, p0, p1):
        diff = mm(gmat[...], split_rows(x))
        diff = diff[: 2 * ROWS] + diff[2 * ROWS :]
        x_i, x_j = diff[:ROWS], diff[ROWS:]
        g = [pair(geo, k, p0, p1) for k in range(4)]
        return x_i, x_j, g[0] * x_i + g[1] * x_j, g[1] * x_i + g[2] * x_j, g[3]

    lam2 = jnp.concatenate([lam, lam], axis=1)

    def weights(r):
        return jnp.concatenate([wts[r], wts[r]], axis=1)

    def apply(c, cols):
        def step(r, carry):
            p0, p1 = r * AZ + cols[0], r * AZ + cols[1]
            x = pair(bf, c, p0, p1)
            x_i, x_j, f_i, f_j, jw = fluxes(x, p0, p1)
            high, low = split(jnp.concatenate([f_i, f_j], axis=0))
            top = mm(dmat[...], high)
            y = top[:ROWS] + top[KROWS : KROWS + ROWS] + mm(dmat[0:KROWS, :], low)[:ROWS]
            y = y + lam2 * jw * x
            yf[c, p0] = y[:, :LANES]
            yf[c, p1] = y[:, LANES:]
            acc[c, 0] = acc[c, 0] + fold(x * x * weights(r))
            acc[c, 1] = acc[c, 1] + fold(x * y)
            return carry

        lax.fori_loop(0, RAD, step, 0)

    def energy(c, cols):
        def step(r, carry):
            p0, p1 = r * AZ + cols[0], r * AZ + cols[1]
            y = pair(yf, c, p0, p1)
            y_i, y_j, f_i, f_j, jw = fluxes(y, p0, p1)
            acc[c, 2] = acc[c, 2] + fold(y * y * weights(r))
            acc[c, 3] = acc[c, 3] + fold(f_i * y_i + f_j * y_j + lam2 * jw * y * y)
            return carry

        lax.fori_loop(0, RAD, step, 0)

    def rhs(c):
        def step(p, carry):
            bf[c, p] = (SIGMA * geo[3, p]) * snd[p, c] - rv2[p, c]
            return carry

        lax.fori_loop(0, ELEMS, step, 0)

    inside, outside = (1, 2), (0, AZ - 1)
    flights = []
    for c in range(2):
        rhs(c)
        flights.append(assemble_start(bf, c, 0))
    for c in range(2):
        apply(c, inside)
    next_flights = []
    for c in range(2):
        assemble_finish(bf, c, 0, flights[c])
        apply(c, outside)
        next_flights.append(assemble_start(yf, c, 1))
    for c in range(2):
        energy(c, inside)
    for c in range(2):
        assemble_finish(yf, c, 1, next_flights[c])
        energy(c, outside)

    sums = jnp.concatenate(
        [jnp.sum(acc[c, k], axis=0, keepdims=True) for c in range(2) for k in range(4)], axis=0
    )

    def exchange(value, slot, group, send_sem, recv_sem, ranks, mine_at, to_device):
        part[slot] = value
        copies = []
        for k, (peer, at) in enumerate(ranks):
            copy = pltpu.make_async_remote_copy(
                src_ref=part.at[slot],
                dst_ref=group.at[mine_at],
                send_sem=send_sem.at[k],
                recv_sem=recv_sem.at[mine_at],
                device_id=(peer, me),
                device_id_type=MESH,
            )
            copy.start()
            copies.append(copy)
        total = value
        for k, (peer, at) in enumerate(ranks):
            pltpu.make_async_remote_copy(
                src_ref=part.at[slot],
                dst_ref=group.at[at],
                send_sem=send_sem.at[k],
                recv_sem=recv_sem.at[at],
                device_id=(peer, me),
                device_id_type=MESH,
            ).wait_recv()
        group[mine_at] = value
        total = group[0]
        for at in range(1, len(ranks) + 1):
            total = total + group[at]
        return total, copies

    z_ranks = [(peer, peer % ZRING) for peer in z_peers]
    y_ranks = [(peer, peer // ZRING) for peer in y_peers]
    sums, more = exchange(sums, 0, gat_z, as_z, ar_z, z_ranks, zed, None)
    halo_sends.extend(more)
    if y_ranks:
        sums, more = exchange(sums, 1, gat_y, as_y, ar_y, y_ranks, why, None)
        halo_sends.extend(more)

    for c in range(2):
        m0, m1, m2, m3 = (sums[c * 4 + k : c * 4 + k + 1] for k in range(4))
        alpha = m0 / m1
        grown = alpha * alpha * m2 - m0
        scale = 1.0 + grown / m0
        below = scale * scale * m1 - 2.0 * scale * alpha * m2 + alpha * alpha * m3
        beyond = grown / below
        on_b = alpha + beyond * scale
        on_y = -beyond * alpha

        def combine(p, carry, c=c, on_b=on_b, on_y=on_y):
            out[c, p] = on_b * bf[c, p] + on_y * yf[c, p]
            return carry

        lax.fori_loop(0, ELEMS, combine, 0)

    for copy in sends + ret_sends + halo_sends:
        copy.wait_send()


def scatter_kernel(slots, grid, out_x, out_y):
    for p in range(ELEMS):
        slot = slots[p]
        out_x[pl.ds(slot, NODES, stride=ELEMS), :] = grid[0, p, 0:NODES]
        out_y[pl.ds(slot, NODES, stride=ELEMS), :] = grid[1, p, 0:NODES]


def body(size_e, vel_x, vel_y, metrics, slot_order):
    there, back, gmat, dmat = constants()
    any_space = pl.BlockSpec(memory_space=pl.ANY)
    vmem = pl.BlockSpec(memory_space=pltpu.VMEM)
    smem = pl.BlockSpec(memory_space=pltpu.SMEM)
    dma = pltpu.SemaphoreType.DMA
    size_y = size_e // ZRING
    rows = NODES * ELEMS
    grid = pl.pallas_call(
        functools.partial(kernel, size_e),
        out_shape=jax.ShapeDtypeStruct((2, ELEMS, ROWS, LANES), F32),
        in_specs=[any_space] * 3 + [smem] + [any_space] * 4,
        out_specs=vmem,
        scratch_shapes=[
            pltpu.VMEM((2, rows, LANES), F32),
            pltpu.VMEM((8, NODES, ELEMS), F32),
            pltpu.VMEM(there.shape, BF16),
            pltpu.VMEM(back.shape, BF16),
            pltpu.VMEM(gmat.shape, BF16),
            pltpu.VMEM(dmat.shape, BF16),
            pltpu.VMEM((ELEMS, 2, ROWS, LANES), F32),
            pltpu.VMEM((GROUPS, 2, 2, ROWS, LANES), F32),
            pltpu.VMEM((4 * ROWS, MODES), BF16),
            pltpu.VMEM((4 * ROWS, PLANES), BF16),
            pltpu.VMEM((2, PLANES // CHUNK, 16, CHUNK), F32),
            pltpu.VMEM((2, 4, ROWS, LANES), F32),
            pltpu.VMEM((4, ELEMS, ROWS, LANES), F32),
            pltpu.VMEM((RAD, ROWS, LANES), F32),
            pltpu.VMEM((2, GROUPS, 2, ROWS, LANES), F32),
            pltpu.VMEM((ELEMS, 2, ROWS, LANES), F32),
            pltpu.VMEM((2, ELEMS, ROWS, LANES), F32),
            pltpu.VMEM((2, ELEMS, ROWS, LANES), F32),
            pltpu.VMEM((2, 2, 2, RAD, 16, LANES), F32),
            pltpu.VMEM((2, 2, 2, RAD, 16, LANES), F32),
            pltpu.VMEM((2, 4, 8, LANES), F32),
            pltpu.VMEM((2, 8, LANES), F32),
            pltpu.VMEM((ZRING, 8, LANES), F32),
            pltpu.VMEM((size_y, 8, LANES), F32),
            dma((7,)),
            dma((2, GROUPS)),
            dma((2, GROUPS)),
            dma((4,)),
            dma((2, GROUPS)),
            dma((2, GROUPS)),
            dma((2, 2, 2)),
            dma((2, 2, 2)),
            dma((ZRING,)),
            dma((ZRING,)),
            dma((size_y,)),
            dma((size_y,)),
        ],
        compiler_params=pltpu.CompilerParams(
            collective_id=0, has_side_effects=True, vmem_limit_bytes=56 * 2**20
        ),
    )(
        vel_x.reshape(rows, LANES),
        vel_y.reshape(rows, LANES),
        metrics,
        slot_order,
        jnp.asarray(there),
        jnp.asarray(back),
        jnp.asarray(gmat),
        jnp.asarray(dmat),
    )
    out_x, out_y = pl.pallas_call(
        scatter_kernel,
        out_shape=[jax.ShapeDtypeStruct((rows, LANES), F32)] * 2,
        in_specs=[smem, vmem],
        out_specs=[vmem, vmem],
        compiler_params=pltpu.CompilerParams(vmem_limit_bytes=32 * 2**20),
    )(slot_order, grid)
    shape = (NODES, ELEMS, LANES)
    return out_x.reshape(shape), out_y.reshape(shape)


def solution(mesh):
    placed = (P(None, "elem", "mode"), P(None, "elem", "mode"), P(None, None, "elem"), P("elem"))
    return jax.shard_map(
        functools.partial(body, mesh.shape["elem"]),
        mesh=mesh,
        in_specs=placed,
        out_specs=(P(None, "elem", "mode"), P(None, "elem", "mode")),
        check_vma=False,
    )
```

time: 541 us -> 74.2 us (0.14); the launches traced: 533 us -> 74 us
  blocking collectives: 218 us -> 0 us
  matrix products: 94.2 us -> 0 us
  Pallas kernels: 0 us -> 70.3 us
  local copies, waits for them, and re-layouts: 70.1 us -> 3.12 us
  waiting for transfers between devices: 66.3 us -> 0 us
  other arithmetic: 61.2 us -> 0 us
  starting transfers between devices: 21.6 us -> 0 us
    psum x3 -> x0, blocking collectives: 218 us -> none  [the longest x2 146 us: squares(): return lax.psum(inner(vector, vector, weight), 'elem')]
    dot_general x17 -> x0, matrix products: 94.2 us -> none  [the longest x1 34.9 us: body(): jnp.dot(products, table.T, precision=HIGH).reshape(2, nodes, share, MODES)]
    pallas_call x0 -> x2, Pallas kernels: none -> 70.3 us  [the longest x1 68 us: body(): pl.pallas_call(functools.partial(kernel, size_e), out_shape=jax.ShapeDtyp...]
    all_to_all x2 -> x0, waiting for transfers between devices: 42.7 us -> none  [the longest x1 23.1 us: body(): lax.all_to_all(spectral, 'mode', split_axis=3, concat_axis=2, tiled=True)]
    dot_general x2 -> x0, other arithmetic: 28.8 us -> none  [the longest x1 28.6 us: body(): jnp.dot(arrived.reshape(-1, MODES), table, precision=HIGH)]
    scatter x7 -> x0, local copies, waits for them, and re-layouts: 28.3 us -> none  [the longest x6 28.1 us: assemble_sector(): field = field.at[:, last, :, :-1].set(joined).at[:, 0, :, 1:].set(joined)]
    ppermute x6 -> x0, waiting for transfers between devices: 23.6 us -> none  [the longest x3 17.5 us: padded_2(): before = lax.ppermute(last, axis, up)]
    all_to_all x2 -> x0, starting transfers between devices: 12.7 us -> none  [the longest x1 6.85 us: body(): lax.all_to_all(stacked, 'mode', split_axis=2, concat_axis=3, tiled=True)]
  transfers between devices with their start and end apart: 8 -> 0, of which waited for: 8 -> 0; matrix products, arithmetic and copies ran while one was open for 7% -> 0% of each run, Pallas kernels for 0% -> 0%
where the time goes in v1:
time: 74.2 us; the launch traced here: 74 us
  Pallas kernels  70.3 us (95%)
  local copies, waits for them, and re-layouts  3.12 us (4%)
    pallas_call x1, Pallas kernels, body(): pl.pallas_call(functools.partial(kernel, size_e), out_shape=jax.ShapeDtyp...  68 us
    unnamed x5, local copies, waits for them, and re-layouts  3.12 us
    pallas_call x1, Pallas kernels, body(): pl.pallas_call(scatter_kernel, out_shape=[jax.ShapeDtypeStruct((rows, LAN...  2.29 us

profile of v1, /device:TPU:2, one launch (start us, length us, event | category | flops | bytes accessed | tf_op | source)
XLA Modules:
  0.0 74.0 jit_solution(13660399134806839130)
XLA Ops:
  0.6 1.8 %copy.10.met_hbm = f32[8,81,16]{2,1,0:T(8,128)} copy(f32[8,81,16]{1,2,0:T(8,128)} %param.10) | data formatting | bytes 82944 | tf_op args[2]
  2.4 0.0 copy-start.1
  2.4 68.0 %shard_map.95.grid = f32[2,16,88,128]{3,2,1,0:T(8,128)} custom-call(f32[1296,128]{1,0:T(8,128)} %bitcast.4, f32[1296,128]{1,0:T(8,128)} %bitcast.5, f32[8,81,16]{2,1,0:T(8,128)} %copy.10.met_hbm, s32[16]{0:T(128)} %slots.3, bf16[2,6,1024,256]{3,2,1,0:T(8,128)(2,1)} %constant.8.clone.there_hbm, bf16[2,4,1536,256]{3,2,1,0:T(8,128)(2,1)} %constant.9.clone.back_hbm, ...), custom_call_target="tpu_custom_call" | custom-call | tf_op jit(solution)/shard_map/pallas_call | solution.py:612
  70.4 0.0 copy-done.1
  70.4 0.0 copy-start
  70.4 1.4 %copy-done = f32[2,16,88,128]{3,2,1,0:T(8,128)S(1)} copy-done((f32[2,16,88,128]{3,2,1,0:T(8,128)S(1)}, f32[2,16,88,128]{3,2,1,0:T(8,128)}, u32[]{:S(2)}) %copy-start) | copy-done | bytes 1441816
  71.7 2.3 %shard_map.96 = (f32[1296,128]{1,0:T(8,128)}, f32[1296,128]{1,0:T(8,128)}) custom-call(s32[16]{0:T(128)S(1)} %copy-done.1, f32[2,16,88,128]{3,2,1,0:T(8,128)S(1)} %copy-done), custom_call_target="tpu_custom_call" | custom-call | tf_op jit(solution)/shard_map/pallas_call | solution.py:668
Async XLA Ops:
  2.4 68.0 %copy-start.1 = (s32[16]{0:T(128)S(1)}, s32[16]{0:T(128)}, u32[]{:S(2)}) copy-start(s32[16]{0:T(128)} %slots.3) | copy-start | bytes 196
  70.4 1.4 %copy-start = (f32[2,16,88,128]{3,2,1,0:T(8,128)S(1)}, f32[2,16,88,128]{3,2,1,0:T(8,128)}, u32[]{:S(2)}) copy-start(f32[2,16,88,128]{3,2,1,0:T(8,128)} %shard_map.95.grid) | copy-start | bytes 4325380

commit v2 on v1

--- a/solution.py
+++ b/solution.py
@@ -126,7 +126,8 @@
 
 
 def position(rank, second):
-    return ((rank % 2) * 2 + second) * AZ + rank // 2
+    row, side = rank // 2, rank % 2
+    return row * AZ + (1 + side if second else (AZ - 1) * side)
 
 
 def kernel(
@@ -150,7 +151,6 @@
     rv,
     act,
     wave,
-    edge,
     pgeo,
     geo,
     wts,
@@ -188,8 +188,9 @@
         (((chip + dc) % 4) * 2 + (core + cc) % 2)
         for dc, cc in ((2, 0), (2, 1), (1, 0), (3, 0), (1, 1), (3, 1), (0, 1))
     ]
-    z_peers = [why * ZRING + (zed + k) % ZRING for k in range(1, ZRING)]
-    y_peers = [((why + k) % size_y) * ZRING + zed for k in range(1, size_y)]
+    z_peers = [why * ZRING + (zed + k) % ZRING for k in (4, 3, 5, 2, 6, 1, 7)]
+    y_hops = sorted(range(1, size_y), key=lambda k: -min(k, size_y - k))
+    y_peers = [((why + k) % size_y) * ZRING + zed for k in y_hops]
 
     loads = [
         pltpu.make_async_copy(velx_hbm, vel.at[0], in_sem.at[0]),
@@ -200,15 +201,14 @@
         pltpu.make_async_copy(there_hbm, there, in_sem.at[5]),
         pltpu.make_async_copy(back_hbm, back, in_sem.at[6]),
     ]
-    for copy in loads:
+    for copy in loads[:5]:
         copy.start()
 
     tail = jnp.zeros((2, 8, LANES), F32)
     for p in range(ELEMS):
         snd[p, :, ROWS - 8 :, :] = tail
         rv[p // 2, p % 2, :, ROWS - 8 :, :] = tail
-        rv2[p, :, EDGE : EDGE + 8, :] = tail
-        rv2[p, :, EDGE + 8 :, :] = tail
+        rv2[p, :, ROWS - 8 :, :] = tail
 
     barrier = pltpu.get_barrier_semaphore()
     for peer in peers:
@@ -262,6 +262,9 @@
                 )
             )
 
+    loads[5].start()
+    loads[6].start()
+
     loads[2].wait()
     loads[3].wait()
     loads[4].wait()
@@ -271,8 +274,8 @@
         return jnp.where(row16 == slots[p], 1.0, 0.0).astype(BF16)
 
     def spread(factors, pick):
-        gap = jnp.zeros((ROWS - NODES, ELEMS), F32)
-        full = jnp.concatenate([factors, gap], axis=0)
+        gap = jnp.zeros((ELEMS, ROWS - NODES), F32)
+        full = jnp.concatenate([factors, gap], axis=1).T
         high = full.astype(BF16)
         rest = full - high.astype(F32)
         mid = rest.astype(BF16)
@@ -312,8 +315,16 @@
 
     acc[...] = jnp.zeros_like(acc)
 
+    def prior(p, carry):
+        twice = SIGMA * geo[3, p]
+        for c in range(2):
+            bf[c, p] = twice * snd[p, c]
+        return carry
+
+    lax.fori_loop(0, ELEMS, prior, 0)
+
     ret_sends = []
-    ret_locals = []
+    ret_locals = [[], []]
     for e in range(2):
         for copy in arrivals[e]:
             copy.wait_recv()
@@ -338,74 +349,57 @@
             for c in range(2):
                 cols = slice(c * CHUNK, (c + 1) * CHUNK)
                 prod = by_i * diff[:ROWS, cols] + by_j * diff[ROWS:, cols]
-                if e == 0:
-                    edge[c, z] = prod[EDGE:]
-                else:
-                    lower = prod[:16] + edge[c, z]
-                    prod = jnp.concatenate([lower, prod[16:]], axis=0)
-                if c == 0:
-                    keep = prod
-            high, low = split(jnp.concatenate([keep, prod], axis=0))
-            at = pl.ds(pl.multiple_of(z * CHUNK, CHUNK), CHUNK)
-            wave[0 : 2 * ROWS, at] = high
-            wave[2 * ROWS :, at] = low
+                at = pl.ds(pl.multiple_of(z * CHUNK, CHUNK), CHUNK)
+                wave[c * 2 * KROWS : (c + 1) * 2 * KROWS, at] = split_rows(prod)
             return carry
 
-        lax.fori_loop(0, PLANES // CHUNK, planes, 0)
+        lax.fori_loop(0, PLANES // CHUNK, planes, 0, unroll=3)
         if e == 0:
             loads[6].wait()
 
-        count = EDGE if e == 0 else NODES
-        for step, dc in enumerate((2, 1, 3, 0)):
-            n = (chip + dc) % 4
-            top = mm(wave[...], back[0, n])
-            hat = top[: 2 * ROWS] + top[2 * ROWS :] + mm(wave[0 : 2 * ROWS, :], back[1, n])
-            for cc in range(2):
-                pass
-            for half in range(2):
-                ret[e, n * 2 + half] = hat[:, half * LANES : (half + 1) * LANES].reshape(2, ROWS, LANES)
-            for cc in range(2):
-                peer = n * 2 + (core + cc) % 2
-                src = ret.at[e, peer, :, pl.ds(0, count)]
-                dst = rv2.at[position(me, e), :, pl.ds(0, count)]
-                if dc == 0 and cc == 0:
-                    copy = pltpu.make_async_copy(src, dst, own.at[2 + e])
-                    ret_locals.append(copy)
-                else:
-                    copy = pltpu.make_async_remote_copy(
-                        src_ref=src,
-                        dst_ref=dst,
-                        send_sem=s2.at[e, step * 2 + cc],
-                        recv_sem=r2.at[e, me],
-                        device_id=(me_e, peer),
-                        device_id_type=MESH,
-                    )
-                    ret_sends.append(copy)
-                copy.start()
-
-    ret_arrivals = []
-    for e in range(2):
-        count = EDGE if e == 0 else NODES
+        for c in range(2):
+            for step, dc in enumerate((2, 1, 3, 0)):
+                n = (chip + dc) % 4
+                top = mm(wave[c * 2 * KROWS : (c + 1) * 2 * KROWS, :], back[0, n])
+                low = mm(wave[c * 2 * KROWS : c * 2 * KROWS + KROWS, :], back[1, n])
+                hat = top[:ROWS] + top[KROWS : KROWS + ROWS] + low[:ROWS]
+                for half in range(2):
+                    ret[e, n * 2 + half, c] = hat[:, half * LANES : (half + 1) * LANES]
+                for cc in range(2):
+                    peer = n * 2 + (core + cc) % 2
+                    src = ret.at[e, peer, c, pl.ds(0, NODES)]
+                    dst = rv2.at[position(me, e), c, pl.ds(0, NODES)]
+                    if dc == 0 and cc == 0:
+                        copy = pltpu.make_async_copy(src, dst, own.at[2 + 2 * e + c])
+                        ret_locals[c].append(copy)
+                    else:
+                        copy = pltpu.make_async_remote_copy(
+                            src_ref=src,
+                            dst_ref=dst,
+                            send_sem=s2.at[e, c, step * 2 + cc],
+                            recv_sem=r2.at[e, c, me],
+                            device_id=(me_e, peer),
+                            device_id_type=MESH,
+                        )
+                        ret_sends.append(copy)
+                    copy.start()
+
+    def wait_returns(e, c):
         for peer in peers:
-            ret_arrivals.append(
-                pltpu.make_async_remote_copy(
-                    src_ref=ret.at[e, 0, :, pl.ds(0, count)],
-                    dst_ref=rv2.at[position(peer, e), :, pl.ds(0, count)],
-                    send_sem=s2.at[e, 0],
-                    recv_sem=r2.at[e, peer],
-                    device_id=(me_e, peer),
-                    device_id_type=MESH,
-                )
-            )
-    for copy in ret_arrivals:
-        copy.wait_recv()
-    for copy in ret_locals:
-        copy.wait()
+            pltpu.make_async_remote_copy(
+                src_ref=ret.at[e, 0, c, pl.ds(0, NODES)],
+                dst_ref=rv2.at[position(peer, e), c, pl.ds(0, NODES)],
+                send_sem=s2.at[e, c, 0],
+                recv_sem=r2.at[e, c, peer],
+                device_id=(me_e, peer),
+                device_id_type=MESH,
+            ).wait_recv()
+        ret_locals[c][e].wait()
 
     halo_sends = []
 
-    def assemble_start(field, c, which):
-        def column(a, carry):
+    def radial(field, c, cols):
+        for a in cols:
             for r in range(RAD - 1):
                 up, down = r * AZ + a, (r + 1) * AZ + a
                 joined = field[c, up, EDGE : EDGE + 8] + field[c, down, 0:8]
@@ -419,12 +413,14 @@
             end = (RAD - 1) * AZ + a
             field[c, end, EDGE : EDGE + 8] = jnp.zeros((8, LANES), F32)
             field[c, end, EDGE + 8 : NODES] = jnp.zeros((1, LANES), F32)
-            return carry
-
-        lax.fori_loop(0, AZ, column, 0)
+
+    first_edge = pl.ds(0, NP, stride=NP)
+    last_edge = pl.ds(NP - 1, NP, stride=NP)
+
+    def rims_start(field, c, which):
         for r in range(RAD):
-            hs[which, c, 0, r, 0:NP] = field[c, r * AZ, pl.ds(0, NP, stride=NP), :]
-            hs[which, c, 1, r, 0:NP] = field[c, r * AZ + AZ - 1, pl.ds(NP - 1, NP, stride=NP), :]
+            hs[which, c, 0, r, 0:NP] = field[c, r * AZ, first_edge, :]
+            hs[which, c, 1, r, 0:NP] = field[c, r * AZ + AZ - 1, last_edge, :]
         copies = []
         for side, peer in ((0, left), (1, right)):
             copy = pltpu.make_async_remote_copy(
@@ -438,31 +434,24 @@
             copy.start()
             copies.append(copy)
         halo_sends.extend(copies)
-
-        def joints(r, carry):
+        return copies
+
+    def joints(field, c):
+        for r in range(RAD):
             for a in range(AZ - 1):
                 p = r * AZ + a
-                shared = (
-                    field[c, p, pl.ds(NP - 1, NP, stride=NP), :]
-                    + field[c, p + 1, pl.ds(0, NP, stride=NP), :]
-                )
-                field[c, p, pl.ds(NP - 1, NP, stride=NP), :] = shared
-                field[c, p + 1, pl.ds(0, NP, stride=NP), :] = shared
-            return carry
-
-        lax.fori_loop(0, RAD, joints, 0)
-        return copies
-
-    def assemble_finish(field, c, which, copies):
+                shared = field[c, p, last_edge, :] + field[c, p + 1, first_edge, :]
+                field[c, p, last_edge, :] = shared
+                field[c, p + 1, first_edge, :] = shared
+
+    def rims_finish(field, c, which, copies):
         for copy in copies:
             copy.wait_recv()
         for r in range(RAD):
             p = r * AZ + AZ - 1
-            at = pl.ds(NP - 1, NP, stride=NP)
-            field[c, p, at, :] = field[c, p, at, :] + hr[which, c, 0, r, 0:NP]
+            field[c, p, last_edge, :] = field[c, p, last_edge, :] + hr[which, c, 0, r, 0:NP]
             p = r * AZ
-            at = pl.ds(0, NP, stride=NP)
-            field[c, p, at, :] = field[c, p, at, :] + hr[which, c, 1, r, 0:NP]
+            field[c, p, first_edge, :] = field[c, p, first_edge, :] + hr[which, c, 1, r, 0:NP]
 
     def pair(ref, c, p0, p1):
         return jnp.concatenate([ref[c, p0], ref[c, p1]], axis=1)
@@ -494,7 +483,7 @@
             acc[c, 1] = acc[c, 1] + fold(x * y)
             return carry
 
-        lax.fori_loop(0, RAD, step, 0)
+        lax.fori_loop(0, RAD, step, 0, unroll=4)
 
     def energy(c, cols):
         def step(r, carry):
@@ -505,32 +494,38 @@
             acc[c, 3] = acc[c, 3] + fold(f_i * y_i + f_j * y_j + lam2 * jw * y * y)
             return carry
 
-        lax.fori_loop(0, RAD, step, 0)
-
-    def rhs(c):
-        def step(p, carry):
-            bf[c, p] = (SIGMA * geo[3, p]) * snd[p, c] - rv2[p, c]
-            return carry
-
-        lax.fori_loop(0, ELEMS, step, 0)
+        lax.fori_loop(0, RAD, step, 0, unroll=4)
+
+    def rhs(c, cols):
+        for r in range(RAD):
+            for a in cols:
+                p = r * AZ + a
+                bf[c, p] = bf[c, p] - rv2[p, c]
+        radial(bf, c, cols)
 
     inside, outside = (1, 2), (0, AZ - 1)
-    flights = []
+    b_flights, y_flights = [], []
     for c in range(2):
-        rhs(c)
-        flights.append(assemble_start(bf, c, 0))
+        wait_returns(0, c)
+        rhs(c, outside)
+        b_flights.append(rims_start(bf, c, 0))
     for c in range(2):
+        wait_returns(1, c)
+        rhs(c, inside)
+        joints(bf, c)
+        rims_finish(bf, c, 0, b_flights[c])
+        apply(c, outside)
+        radial(yf, c, outside)
+        y_flights.append(rims_start(yf, c, 1))
         apply(c, inside)
-    next_flights = []
-    for c in range(2):
-        assemble_finish(bf, c, 0, flights[c])
-        apply(c, outside)
-        next_flights.append(assemble_start(yf, c, 1))
-    for c in range(2):
-        energy(c, inside)
-    for c in range(2):
-        assemble_finish(yf, c, 1, next_flights[c])
-        energy(c, outside)
+        radial(yf, c, inside)
+        joints(yf, c)
+    energy(0, inside)
+    rims_finish(yf, 0, 1, y_flights[0])
+    energy(0, outside)
+    energy(1, inside)
+    rims_finish(yf, 1, 1, y_flights[1])
+    energy(1, outside)
 
     sums = jnp.concatenate(
         [jnp.sum(acc[c, k], axis=0, keepdims=True) for c in range(2) for k in range(4)], axis=0
@@ -611,12 +606,12 @@
     rows = NODES * ELEMS
     grid = pl.pallas_call(
         functools.partial(kernel, size_e),
-        out_shape=jax.ShapeDtypeStruct((2, ELEMS, ROWS, LANES), F32),
+        out_shape=pltpu.VMEM((2, ELEMS, ROWS, LANES), F32),
         in_specs=[any_space] * 3 + [smem] + [any_space] * 4,
         out_specs=vmem,
         scratch_shapes=[
             pltpu.VMEM((2, rows, LANES), F32),
-            pltpu.VMEM((8, NODES, ELEMS), F32),
+            pltpu.VMEM((8, ELEMS, NODES), F32),
             pltpu.VMEM(there.shape, BF16),
             pltpu.VMEM(back.shape, BF16),
             pltpu.VMEM(gmat.shape, BF16),
@@ -624,8 +619,7 @@
             pltpu.VMEM((ELEMS, 2, ROWS, LANES), F32),
             pltpu.VMEM((GROUPS, 2, 2, ROWS, LANES), F32),
             pltpu.VMEM((4 * ROWS, MODES), BF16),
-            pltpu.VMEM((4 * ROWS, PLANES), BF16),
-            pltpu.VMEM((2, PLANES // CHUNK, 16, CHUNK), F32),
+            pltpu.VMEM((4 * KROWS, PLANES), BF16),
             pltpu.VMEM((2, 4, ROWS, LANES), F32),
             pltpu.VMEM((4, ELEMS, ROWS, LANES), F32),
             pltpu.VMEM((RAD, ROWS, LANES), F32),
@@ -642,9 +636,9 @@
             dma((7,)),
             dma((2, GROUPS)),
             dma((2, GROUPS)),
-            dma((4,)),
-            dma((2, GROUPS)),
-            dma((2, GROUPS)),
+            dma((6,)),
+            dma((2, 2, GROUPS)),
+            dma((2, 2, GROUPS)),
             dma((2, 2, 2)),
             dma((2, 2, 2)),
             dma((ZRING,)),
@@ -658,7 +652,7 @@
     )(
         vel_x.reshape(rows, LANES),
         vel_y.reshape(rows, LANES),
-        metrics,
+        metrics.transpose(0, 2, 1),
         slot_order,
         jnp.asarray(there),
         jnp.asarray(back),

time: 74.2 us -> 61.3 us (0.83); the launches traced: 74 us -> 60.3 us
  Pallas kernels: 70.3 us -> 59.7 us
  local copies, waits for them, and re-layouts: 3.12 us -> 0.01 us
    pallas_call x1, Pallas kernels: 68 us -> 57.4 us  [body(): pl.pallas_call(functools.partial(kernel, size_e), out_shape=pltpu.VMEM((2...]
    unnamed x5 -> x2, local copies, waits for them, and re-layouts: 3.12 us -> 0.01 us
where the time goes in v2:
time: 61.3 us; the launch traced here: 60.3 us
  Pallas kernels  59.7 us (97%)
  between operations  0.65 us (1%)
    pallas_call x1, Pallas kernels, body(): pl.pallas_call(functools.partial(kernel, size_e), out_shape=pltpu.VMEM((2...  57.4 us
    pallas_call x1, Pallas kernels, body(): pl.pallas_call(scatter_kernel, out_shape=[jax.ShapeDtypeStruct((rows, LAN...  2.3 us

profile of v2, /device:TPU:2, one launch (start us, length us, event | category | flops | bytes accessed | tf_op | source)
XLA Modules:
  0.0 60.3 jit_solution(6227950916255264527)
XLA Ops:
  0.6 0.0 copy-start
  0.6 57.4 %shard_map.95.grid = f32[2,16,88,128]{3,2,1,0:T(8,128)S(1)} custom-call(f32[1296,128]{1,0:T(8,128)} %bitcast.5, f32[1296,128]{1,0:T(8,128)} %bitcast.6, f32[8,16,81]{2,1,0:T(8,128)} %bitcast.7, s32[16]{0:T(128)} %slots.3, bf16[2,6,1024,256]{3,2,1,0:T(8,128)(2,1)} %constant.8.clone.there_hbm, bf16[2,4,1536,256]{3,2,1,0:T(8,128)(2,1)} %constant.9.clone.back_hbm, ...), custom_call_target="tpu_custom_call" | custom-call | tf_op jit(solution)/shard_map/pallas_call | solution.py:607
  58.0 0.0 copy-done
  58.0 2.3 %shard_map.96 = (f32[1296,128]{1,0:T(8,128)}, f32[1296,128]{1,0:T(8,128)}) custom-call(s32[16]{0:T(128)S(1)} %copy-done, f32[2,16,88,128]{3,2,1,0:T(8,128)S(1)} %shard_map.95.grid), custom_call_target="tpu_custom_call" | custom-call | tf_op jit(solution)/shard_map/pallas_call | solution.py:662
Async XLA Ops:
  0.6 57.4 %copy-start = (s32[16]{0:T(128)S(1)}, s32[16]{0:T(128)}, u32[]{:S(2)}) copy-start(s32[16]{0:T(128)} %slots.3) | copy-start | bytes 196

commit v3 on v2

--- a/solution.py
+++ b/solution.py
@@ -140,7 +140,8 @@
     back_hbm,
     gmat_hbm,
     dmat_hbm,
-    out,
+    out_x,
+    out_y,
     vel,
     met,
     there,
@@ -162,8 +163,7 @@
     hr,
     acc,
     part,
-    gat_z,
-    gat_y,
+    gat,
     in_sem,
     s1,
     r1,
@@ -172,11 +172,16 @@
     r2,
     hsem,
     hrem,
-    as_z,
-    ar_z,
-    as_y,
-    ar_y,
+    as_all,
+    ar_all,
+    known,
+    inverse,
+    esnd,
+    ercv,
+    es,
+    er,
 ):
+    outs = (out_x, out_y)
     me_e = lax.axis_index("elem")
     me = lax.axis_index("mode")
     chip, core = me // 2, me % 2
@@ -189,8 +194,16 @@
         for dc, cc in ((2, 0), (2, 1), (1, 0), (3, 0), (1, 1), (3, 1), (0, 1))
     ]
     z_peers = [why * ZRING + (zed + k) % ZRING for k in (4, 3, 5, 2, 6, 1, 7)]
-    y_hops = sorted(range(1, size_y), key=lambda k: -min(k, size_y - k))
-    y_peers = [((why + k) % size_y) * ZRING + zed for k in y_hops]
+    y_peers = [((why + k) % size_y) * ZRING + zed for k in range(1, size_y)]
+
+    def hops(step):
+        return min(step[0], size_y - step[0]) + min(step[1], ZRING - step[1])
+
+    steps = [(dy, dz) for dy in range(size_y) for dz in range(ZRING) if dy or dz]
+    all_peers = [
+        ((why + dy) % size_y) * ZRING + (zed + dz) % ZRING
+        for dy, dz in sorted(steps, key=lambda step: -hops(step))
+    ]
 
     loads = [
         pltpu.make_async_copy(velx_hbm, vel.at[0], in_sem.at[0]),
@@ -217,6 +230,9 @@
         pl.semaphore_signal(barrier, inc=1, device_id=(peer, me), device_id_type=MESH)
 
     pl.semaphore_wait(barrier, len(peers) + len(z_peers) + len(y_peers) + 2)
+
+    for peer in y_peers:
+        pl.semaphore_signal(known, inc=1, device_id=(peer, me), device_id_type=MESH)
 
     loads[0].wait()
     loads[1].wait()
@@ -315,6 +331,13 @@
 
     acc[...] = jnp.zeros_like(acc)
 
+    stored = [slots[p] for p in range(ELEMS)]
+    for s in range(ELEMS):
+        place = jnp.int32(0)
+        for p in range(1, ELEMS):
+            place = jnp.where(stored[p] == s, jnp.int32(p), place)
+        inverse[s] = place
+
     def prior(p, carry):
         twice = SIGMA * geo[3, p]
         for c in range(2):
@@ -325,6 +348,26 @@
 
     ret_sends = []
     ret_locals = [[], []]
+
+    def send_back(e, c):
+        for k, peer in enumerate(peers):
+            copy = pltpu.make_async_remote_copy(
+                src_ref=ret.at[e, peer, c, pl.ds(0, NODES)],
+                dst_ref=rv2.at[position(me, e), c, pl.ds(0, NODES)],
+                send_sem=s2.at[e, c, k],
+                recv_sem=r2.at[e, c, me],
+                device_id=(me_e, peer),
+                device_id_type=MESH,
+            )
+            copy.start()
+            ret_sends.append(copy)
+        copy = pltpu.make_async_copy(
+            ret.at[e, me, c, pl.ds(0, NODES)],
+            rv2.at[position(me, e), c, pl.ds(0, NODES)],
+            own.at[2 + 2 * e + c],
+        )
+        copy.start()
+        ret_locals[c].append(copy)
     for e in range(2):
         for copy in arrivals[e]:
             copy.wait_recv()
@@ -365,24 +408,27 @@
                 hat = top[:ROWS] + top[KROWS : KROWS + ROWS] + low[:ROWS]
                 for half in range(2):
                     ret[e, n * 2 + half, c] = hat[:, half * LANES : (half + 1) * LANES]
-                for cc in range(2):
-                    peer = n * 2 + (core + cc) % 2
-                    src = ret.at[e, peer, c, pl.ds(0, NODES)]
-                    dst = rv2.at[position(me, e), c, pl.ds(0, NODES)]
-                    if dc == 0 and cc == 0:
-                        copy = pltpu.make_async_copy(src, dst, own.at[2 + 2 * e + c])
-                        ret_locals[c].append(copy)
-                    else:
-                        copy = pltpu.make_async_remote_copy(
-                            src_ref=src,
-                            dst_ref=dst,
-                            send_sem=s2.at[e, c, step * 2 + cc],
-                            recv_sem=r2.at[e, c, me],
-                            device_id=(me_e, peer),
-                            device_id_type=MESH,
-                        )
-                        ret_sends.append(copy)
-                    copy.start()
+            if e == 0:
+                send_back(e, c)
+        if e == 1:
+            shared = pl.ds((me % 2) * (NP - 1), NP, stride=NP)
+            for rank in range(GROUPS):
+                for c in range(2):
+                    esnd[rank, c, 0:NP] = ret[1, rank, c, shared, :]
+            for k, peer in enumerate(peers):
+                copy = pltpu.make_async_remote_copy(
+                    src_ref=esnd.at[peer, :, pl.ds(0, NP)],
+                    dst_ref=ercv.at[me, :, pl.ds(0, NP)],
+                    send_sem=es.at[k],
+                    recv_sem=er.at[me],
+                    device_id=(me_e, peer),
+                    device_id_type=MESH,
+                )
+                copy.start()
+                ret_sends.append(copy)
+            for c in range(2):
+                ercv[me, c, 0:NP] = esnd[me, c, 0:NP]
+                send_back(e, c)
 
     def wait_returns(e, c):
         for peer in peers:
@@ -509,65 +555,87 @@
         wait_returns(0, c)
         rhs(c, outside)
         b_flights.append(rims_start(bf, c, 0))
+    for peer in peers:
+        pltpu.make_async_remote_copy(
+            src_ref=esnd.at[peer, :, pl.ds(0, NP)],
+            dst_ref=ercv.at[peer, :, pl.ds(0, NP)],
+            send_sem=es.at[0],
+            recv_sem=er.at[peer],
+            device_id=(me_e, peer),
+            device_id_type=MESH,
+        ).wait_recv()
+
+    seams = ((0, last_edge, 1, first_edge), (AZ - 1, first_edge, AZ - 2, last_edge))
+
+    def outer_seams(c):
+        for side, (outer, edge_o, inner, edge_i) in enumerate(seams):
+            terms = [
+                bf[c, r * AZ + inner, edge_i, :] - ercv[2 * r + side, c, 0:NP] for r in range(RAD)
+            ]
+            zero = jnp.zeros((1, LANES), F32)
+            joins = [zero] + [terms[r][NP - 1 :] + terms[r + 1][:1] for r in range(RAD - 1)] + [zero]
+            for r in range(RAD):
+                whole = jnp.concatenate([joins[r], terms[r][1 : NP - 1], joins[r + 1]], axis=0)
+                p = r * AZ + outer
+                bf[c, p, edge_o, :] = bf[c, p, edge_o, :] + whole
+
+    def inner_joints(c):
+        for r in range(RAD):
+            for outer, edge_o, inner, edge_i in seams:
+                bf[c, r * AZ + inner, edge_i, :] = bf[c, r * AZ + outer, edge_o, :]
+            p = r * AZ + 1
+            shared = bf[c, p, last_edge, :] + bf[c, p + 1, first_edge, :]
+            bf[c, p, last_edge, :] = shared
+            bf[c, p + 1, first_edge, :] = shared
+
     for c in range(2):
-        wait_returns(1, c)
-        rhs(c, inside)
-        joints(bf, c)
+        outer_seams(c)
+    for c in range(2):
         rims_finish(bf, c, 0, b_flights[c])
         apply(c, outside)
         radial(yf, c, outside)
         y_flights.append(rims_start(yf, c, 1))
+    for c in range(2):
+        wait_returns(1, c)
+        rhs(c, inside)
+        inner_joints(c)
         apply(c, inside)
         radial(yf, c, inside)
         joints(yf, c)
-    energy(0, inside)
-    rims_finish(yf, 0, 1, y_flights[0])
-    energy(0, outside)
-    energy(1, inside)
-    rims_finish(yf, 1, 1, y_flights[1])
-    energy(1, outside)
+        energy(c, inside)
+    for c in range(2):
+        rims_finish(yf, c, 1, y_flights[c])
+        energy(c, outside)
 
     sums = jnp.concatenate(
         [jnp.sum(acc[c, k], axis=0, keepdims=True) for c in range(2) for k in range(4)], axis=0
     )
 
-    def exchange(value, slot, group, send_sem, recv_sem, ranks, mine_at, to_device):
-        part[slot] = value
-        copies = []
-        for k, (peer, at) in enumerate(ranks):
-            copy = pltpu.make_async_remote_copy(
-                src_ref=part.at[slot],
-                dst_ref=group.at[mine_at],
-                send_sem=send_sem.at[k],
-                recv_sem=recv_sem.at[mine_at],
-                device_id=(peer, me),
-                device_id_type=MESH,
-            )
-            copy.start()
-            copies.append(copy)
-        total = value
-        for k, (peer, at) in enumerate(ranks):
-            pltpu.make_async_remote_copy(
-                src_ref=part.at[slot],
-                dst_ref=group.at[at],
-                send_sem=send_sem.at[k],
-                recv_sem=recv_sem.at[at],
-                device_id=(peer, me),
-                device_id_type=MESH,
-            ).wait_recv()
-        group[mine_at] = value
-        total = group[0]
-        for at in range(1, len(ranks) + 1):
-            total = total + group[at]
-        return total, copies
-
-    z_ranks = [(peer, peer % ZRING) for peer in z_peers]
-    y_ranks = [(peer, peer // ZRING) for peer in y_peers]
-    sums, more = exchange(sums, 0, gat_z, as_z, ar_z, z_ranks, zed, None)
-    halo_sends.extend(more)
-    if y_ranks:
-        sums, more = exchange(sums, 1, gat_y, as_y, ar_y, y_ranks, why, None)
-        halo_sends.extend(more)
+    part[...] = sums
+    if y_peers:
+        pl.semaphore_wait(known, len(y_peers))
+    for k, peer in enumerate(all_peers):
+        copy = pltpu.make_async_remote_copy(
+            src_ref=part,
+            dst_ref=gat.at[me_e],
+            send_sem=as_all.at[k],
+            recv_sem=ar_all.at[me_e],
+            device_id=(peer, me),
+            device_id_type=MESH,
+        )
+        copy.start()
+        halo_sends.append(copy)
+    gat[me_e] = sums
+    for k, peer in enumerate(all_peers):
+        pltpu.make_async_remote_copy(
+            src_ref=part,
+            dst_ref=gat.at[peer],
+            send_sem=as_all.at[k],
+            recv_sem=ar_all.at[peer],
+            device_id=(peer, me),
+            device_id_type=MESH,
+        ).wait_recv()
+    sums = jnp.sum(gat[...], axis=0)
 
     for c in range(2):
         m0, m1, m2, m3 = (sums[c * 4 + k : c * 4 + k + 1] for k in range(4))
@@ -579,21 +647,16 @@
         on_b = alpha + beyond * scale
         on_y = -beyond * alpha
 
-        def combine(p, carry, c=c, on_b=on_b, on_y=on_y):
-            out[c, p] = on_b * bf[c, p] + on_y * yf[c, p]
+        def combine(s, carry, c=c, on_b=on_b, on_y=on_y):
+            p = inverse[s]
+            grid = on_b * bf[c, p] + on_y * yf[c, p]
+            outs[c][pl.ds(s, NODES, stride=ELEMS), :] = grid[:NODES]
             return carry
 
-        lax.fori_loop(0, ELEMS, combine, 0)
+        lax.fori_loop(0, ELEMS, combine, 0, unroll=4)
 
     for copy in sends + ret_sends + halo_sends:
         copy.wait_send()
-
-
-def scatter_kernel(slots, grid, out_x, out_y):
-    for p in range(ELEMS):
-        slot = slots[p]
-        out_x[pl.ds(slot, NODES, stride=ELEMS), :] = grid[0, p, 0:NODES]
-        out_y[pl.ds(slot, NODES, stride=ELEMS), :] = grid[1, p, 0:NODES]
 
 
 def body(size_e, vel_x, vel_y, metrics, slot_order):
@@ -602,13 +665,12 @@
     vmem = pl.BlockSpec(memory_space=pltpu.VMEM)
     smem = pl.BlockSpec(memory_space=pltpu.SMEM)
     dma = pltpu.SemaphoreType.DMA
-    size_y = size_e // ZRING
     rows = NODES * ELEMS
-    grid = pl.pallas_call(
+    out_x, out_y = pl.pallas_call(
         functools.partial(kernel, size_e),
-        out_shape=pltpu.VMEM((2, ELEMS, ROWS, LANES), F32),
+        out_shape=[pltpu.VMEM((rows, LANES), F32)] * 2,
         in_specs=[any_space] * 3 + [smem] + [any_space] * 4,
-        out_specs=vmem,
+        out_specs=[vmem, vmem],
         scratch_shapes=[
             pltpu.VMEM((2, rows, LANES), F32),
             pltpu.VMEM((8, ELEMS, NODES), F32),
@@ -630,9 +692,8 @@
             pltpu.VMEM((2, 2, 2, RAD, 16, LANES), F32),
             pltpu.VMEM((2, 2, 2, RAD, 16, LANES), F32),
             pltpu.VMEM((2, 4, 8, LANES), F32),
-            pltpu.VMEM((2, 8, LANES), F32),
-            pltpu.VMEM((ZRING, 8, LANES), F32),
-            pltpu.VMEM((size_y, 8, LANES), F32),
+            pltpu.VMEM((8, LANES), F32),
+            pltpu.VMEM((size_e, 8, LANES), F32),
             dma((7,)),
             dma((2, GROUPS)),
             dma((2, GROUPS)),
@@ -641,10 +702,14 @@
             dma((2, 2, GROUPS)),
             dma((2, 2, 2)),
             dma((2, 2, 2)),
-            dma((ZRING,)),
-            dma((ZRING,)),
-            dma((size_y,)),
-            dma((size_y,)),
+            dma((size_e,)),
+            dma((size_e,)),
+            pltpu.SemaphoreType.REGULAR,
+            pltpu.SMEM((ELEMS,), jnp.int32),
+            pltpu.VMEM((GROUPS, 2, 16, LANES), F32),
+            pltpu.VMEM((GROUPS, 2, 16, LANES), F32),
+            dma((GROUPS,)),
+            dma((GROUPS,)),
         ],
         compiler_params=pltpu.CompilerParams(
             collective_id=0, has_side_effects=True, vmem_limit_bytes=56 * 2**20
@@ -659,13 +724,6 @@
         jnp.asarray(gmat),
         jnp.asarray(dmat),
     )
-    out_x, out_y = pl.pallas_call(
-        scatter_kernel,
-        out_shape=[jax.ShapeDtypeStruct((rows, LANES), F32)] * 2,
-        in_specs=[smem, vmem],
-        out_specs=[vmem, vmem],
-        compiler_params=pltpu.CompilerParams(vmem_limit_bytes=32 * 2**20),
-    )(slot_order, grid)
     shape = (NODES, ELEMS, LANES)
     return out_x.reshape(shape), out_y.reshape(shape)
 

time: 61.3 us -> 56.7 us (0.925)
  Pallas kernels: 59.7 us -> 53.6 us
  local copies, waits for them, and re-layouts: 0.01 us -> 1.68 us
    pallas_call x2 -> x1, Pallas kernels: 59.7 us -> 53.6 us  [body(): pl.pallas_call(functools.partial(kernel, size_e), out_shape=[pltpu.VMEM((...]
    unnamed x2, local copies, waits for them, and re-layouts: 0.01 us -> 1.68 us
where the time goes in v3:
time: 56.7 us; the launch traced here: 55.9 us
  Pallas kernels  53.6 us (95%)
  local copies, waits for them, and re-layouts  1.68 us (3%)
  between operations  0.64 us (1%)
    pallas_call x1, Pallas kernels, body(): pl.pallas_call(functools.partial(kernel, size_e), out_shape=[pltpu.VMEM((...  53.6 us
    unnamed x2, local copies, waits for them, and re-layouts  1.68 us

profile of v3, /device:TPU:2, one launch (start us, length us, event | category | flops | bytes accessed | tf_op | source)
XLA Modules:
  0.0 55.9 jit_solution(5188309154417205580)
XLA Ops:
  0.6 53.6 %shard_map.95 = (f32[1296,128]{1,0:T(8,128)S(1)}, f32[1296,128]{1,0:T(8,128)S(1)}) custom-call(f32[1296,128]{1,0:T(8,128)} %bitcast.7, f32[1296,128]{1,0:T(8,128)} %bitcast.8, f32[8,16,81]{2,1,0:T(8,128)} %bitcast.9, s32[16]{0:T(128)} %slots.1, bf16[2,6,1024,256]{3,2,1,0:T(8,128)(2,1)} %constant.8.clone.there_hbm, ...), custom_call_target="tpu_custom_call" | custom-call | tf_op jit(solution)/shard_map/pallas_call | solution.py:669
  54.2 0.8 %copy.12 = f32[81,16,128]{2,1,0:T(8,128)} copy(f32[81,16,128]{2,1,0:T(8,128)S(1)} %bitcast.6) | data formatting | bytes 1327104
  55.1 0.8 %copy.13 = f32[81,16,128]{2,1,0:T(8,128)} copy(f32[81,16,128]{2,1,0:T(8,128)S(1)} %bitcast.5) | data formatting | bytes 1327104

commit v4 on v3

--- a/solution.py
+++ b/solution.py
@@ -27,6 +27,7 @@
 ZRING = 8
 SIGMA = 2.0
 WAVE = 64.0
+PIECES = 2
 MESH = pl.DeviceIdType.MESH
 F32 = jnp.float32
 BF16 = jnp.bfloat16
@@ -140,8 +141,11 @@
     back_hbm,
     gmat_hbm,
     dmat_hbm,
-    out_x,
-    out_y,
+    b_x,
+    b_y,
+    y_x,
+    y_y,
+    coef,
     vel,
     met,
     there,
@@ -157,6 +161,7 @@
     wts,
     ret,
     rv2,
+    pack,
     bf,
     yf,
     hs,
@@ -181,7 +186,7 @@
     es,
     er,
 ):
-    outs = (out_x, out_y)
+    outs_b, outs_y = (b_x, b_y), (y_x, y_y)
     me_e = lax.axis_index("elem")
     me = lax.axis_index("mode")
     chip, core = me // 2, me % 2
@@ -221,7 +226,6 @@
     for p in range(ELEMS):
         snd[p, :, ROWS - 8 :, :] = tail
         rv[p // 2, p % 2, :, ROWS - 8 :, :] = tail
-        rv2[p, :, ROWS - 8 :, :] = tail
 
     barrier = pltpu.get_barrier_semaphore()
     for peer in peers:
@@ -349,11 +353,21 @@
     ret_sends = []
     ret_locals = [[], []]
 
+    side = me % 2
+
     def send_back(e, c):
+        start = 1 - side if e else side
+
+        def pack_rank(rank, carry):
+            for i in range(NP):
+                pack[e, rank, c, 8 * i : 8 * i + 8] = ret[e, rank, c, pl.ds(NP * i + start, 8), :]
+            return carry
+
+        lax.fori_loop(0, GROUPS, pack_rank, 0, unroll=2)
         for k, peer in enumerate(peers):
             copy = pltpu.make_async_remote_copy(
-                src_ref=ret.at[e, peer, c, pl.ds(0, NODES)],
-                dst_ref=rv2.at[position(me, e), c, pl.ds(0, NODES)],
+                src_ref=pack.at[e, peer, c],
+                dst_ref=rv2.at[position(me, e), c],
                 send_sem=s2.at[e, c, k],
                 recv_sem=r2.at[e, c, me],
                 device_id=(me_e, peer),
@@ -362,8 +376,8 @@
             copy.start()
             ret_sends.append(copy)
         copy = pltpu.make_async_copy(
-            ret.at[e, me, c, pl.ds(0, NODES)],
-            rv2.at[position(me, e), c, pl.ds(0, NODES)],
+            pack.at[e, me, c],
+            rv2.at[position(me, e), c],
             own.at[2 + 2 * e + c],
         )
         copy.start()
@@ -411,10 +425,11 @@
             if e == 0:
                 send_back(e, c)
         if e == 1:
-            shared = pl.ds((me % 2) * (NP - 1), NP, stride=NP)
+            near = pl.ds(side * (NP - 1), NP, stride=NP)
+            far = pl.ds((1 - side) * (NP - 1), NP, stride=NP)
             for rank in range(GROUPS):
                 for c in range(2):
-                    esnd[rank, c, 0:NP] = ret[1, rank, c, shared, :]
+                    esnd[rank, c, 0:NP] = ret[1, rank, c, near, :] + ret[0, rank, c, far, :]
             for k, peer in enumerate(peers):
                 copy = pltpu.make_async_remote_copy(
                     src_ref=esnd.at[peer, :, pl.ds(0, NP)],
@@ -433,8 +448,8 @@
     def wait_returns(e, c):
         for peer in peers:
             pltpu.make_async_remote_copy(
-                src_ref=ret.at[e, 0, c, pl.ds(0, NODES)],
-                dst_ref=rv2.at[position(peer, e), c, pl.ds(0, NODES)],
+                src_ref=pack.at[e, 0, c],
+                dst_ref=rv2.at[position(peer, e), c],
                 send_sem=s2.at[e, c, 0],
                 recv_sem=r2.at[e, c, peer],
                 device_id=(me_e, peer),
@@ -546,7 +561,9 @@
         for r in range(RAD):
             for a in cols:
                 p = r * AZ + a
-                bf[c, p] = bf[c, p] - rv2[p, c]
+                for i in range(NP):
+                    at = slice(NP * i + a % 2, NP * i + a % 2 + 8)
+                    bf[c, p, at] = bf[c, p, at] - rv2[p, c, 8 * i : 8 * i + 8]
         radial(bf, c, cols)
 
     inside, outside = (1, 2), (0, AZ - 1)
@@ -626,6 +643,16 @@
         copy.start()
         halo_sends.append(copy)
     gat[me_e] = sums
+    for c in range(2):
+
+        def store(s, carry, c=c):
+            p = inverse[s]
+            at = pl.ds(s, NODES, stride=ELEMS)
+            outs_b[c][at, :] = bf[c, p, 0:NODES]
+            outs_y[c][at, :] = yf[c, p, 0:NODES]
+            return carry
+
+        lax.fori_loop(0, ELEMS, store, 0, unroll=4)
     for k, peer in enumerate(all_peers):
         pltpu.make_async_remote_copy(
             src_ref=part,
@@ -647,16 +674,25 @@
         on_b = alpha + beyond * scale
         on_y = -beyond * alpha
 
-        def combine(s, carry, c=c, on_b=on_b, on_y=on_y):
-            p = inverse[s]
-            grid = on_b * bf[c, p] + on_y * yf[c, p]
-            outs[c][pl.ds(s, NODES, stride=ELEMS), :] = grid[:NODES]
-            return carry
-
-        lax.fori_loop(0, ELEMS, combine, 0, unroll=4)
+        coef[2 * c : 2 * c + 1] = on_b
+        coef[2 * c + 1 : 2 * c + 2] = on_y
 
     for copy in sends + ret_sends + halo_sends:
         copy.wait_send()
+
+
+def combine_kernel(b_x, b_y, y_x, y_y, coef, out_x, out_y, held, sem):
+    size = b_x.shape[0] // PIECES
+    copies = []
+    for piece in range(PIECES):
+        at = pl.ds(piece * size, size)
+        for c, (b, y, out) in enumerate(((b_x, y_x, out_x), (b_y, y_y, out_y))):
+            held[c, at] = coef[2 * c : 2 * c + 1] * b[at] + coef[2 * c + 1 : 2 * c + 2] * y[at]
+            copy = pltpu.make_async_copy(held.at[c, at], out.at[at], sem.at[c, piece])
+            copy.start()
+            copies.append(copy)
+    for copy in copies:
+        copy.wait()
 
 
 def body(size_e, vel_x, vel_y, metrics, slot_order):
@@ -666,11 +702,11 @@
     smem = pl.BlockSpec(memory_space=pltpu.SMEM)
     dma = pltpu.SemaphoreType.DMA
     rows = NODES * ELEMS
-    out_x, out_y = pl.pallas_call(
+    b_x, b_y, y_x, y_y, coef = pl.pallas_call(
         functools.partial(kernel, size_e),
-        out_shape=[pltpu.VMEM((rows, LANES), F32)] * 2,
+        out_shape=[pltpu.VMEM((rows, LANES), F32)] * 4 + [pltpu.VMEM((8, LANES), F32)],
         in_specs=[any_space] * 3 + [smem] + [any_space] * 4,
-        out_specs=[vmem, vmem],
+        out_specs=[vmem] * 5,
         scratch_shapes=[
             pltpu.VMEM((2, rows, LANES), F32),
             pltpu.VMEM((8, ELEMS, NODES), F32),
@@ -686,7 +722,8 @@
             pltpu.VMEM((4, ELEMS, ROWS, LANES), F32),
             pltpu.VMEM((RAD, ROWS, LANES), F32),
             pltpu.VMEM((2, GROUPS, 2, ROWS, LANES), F32),
-            pltpu.VMEM((ELEMS, 2, ROWS, LANES), F32),
+            pltpu.VMEM((ELEMS, 2, NP * ORDER, LANES), F32),
+            pltpu.VMEM((2, GROUPS, 2, NP * ORDER, LANES), F32),
             pltpu.VMEM((2, ELEMS, ROWS, LANES), F32),
             pltpu.VMEM((2, ELEMS, ROWS, LANES), F32),
             pltpu.VMEM((2, 2, 2, RAD, 16, LANES), F32),
@@ -724,6 +761,14 @@
         jnp.asarray(gmat),
         jnp.asarray(dmat),
     )
+    out_x, out_y = pl.pallas_call(
+        combine_kernel,
+        out_shape=[jax.ShapeDtypeStruct((rows, LANES), F32)] * 2,
+        in_specs=[vmem] * 5,
+        out_specs=[any_space] * 2,
+        scratch_shapes=[pltpu.VMEM((2, rows, LANES), F32), dma((2, PIECES))],
+        compiler_params=pltpu.CompilerParams(vmem_limit_bytes=16 * 2**20),
+    )(b_x, b_y, y_x, y_y, coef)
     shape = (NODES, ELEMS, LANES)
     return out_x.reshape(shape), out_y.reshape(shape)
 

time: 56.7 us -> 55.2 us (0.974)
  the two profiles are of different devices: /device:TPU:2 before, /device:TPU:1 now
where the time goes in v4:
time: 55.2 us
  Pallas kernels  54.5 us (99%)
  between operations  0.64 us (1%)
    pallas_call x1, Pallas kernels, body(): pl.pallas_call(functools.partial(kernel, size_e), out_shape=[pltpu.VMEM((...  53.4 us
    pallas_call x1, Pallas kernels, body(): pl.pallas_call(combine_kernel, out_shape=[jax.ShapeDtypeStruct((rows, LAN...  1.13 us

profile of v4, /device:TPU:1, one launch (start us, length us, event | category | flops | bytes accessed | tf_op | source)
XLA Modules:
  0.0 55.2 jit_solution(15215140379286662882)
XLA Ops:
  0.6 53.4 %shard_map.95 = (f32[1296,128]{1,0:T(8,128)S(1)}, f32[1296,128]{1,0:T(8,128)S(1)}, f32[1296,128]{1,0:T(8,128)S(1)}, f32[1296,128]{1,0:T(8,128)S(1)}, f32[8,128]{1,0:T(8,128)S(1)}) custom-call(f32[1296,128]{1,0:T(8,128)} %bitcast.5, f32[1296,128]{1,0:T(8,128)} %bitcast.6, f32[8,16,81]{2,1,0:T(8,128)} %bitcast.7, s32[16]{0:T(128)} %slots.1, ...), custom_call_target="tpu_custom_call" | custom-call | tf_op jit(solution)/shard_map/pallas_call | solution.py:705
  54.0 1.1 %shard_map.96 = (f32[1296,128]{1,0:T(8,128)}, f32[1296,128]{1,0:T(8,128)}) custom-call(f32[1296,128]{1,0:T(8,128)S(1)} %get-tuple-element.9.b_x, f32[1296,128]{1,0:T(8,128)S(1)} %get-tuple-element.10.b_y, f32[1296,128]{1,0:T(8,128)S(1)} %get-tuple-element.11.y_x, f32[1296,128]{1,0:T(8,128)S(1)} %get-tuple-element.12.y_y, f32[8,128]{1,0:T(8,128)S(1)} %get-tuple-element.13.coef), custom_call_target="tpu_custom_call" | custom-call | tf_op jit(solution)/shard_map/pallas_call | solution.py:764

commit v5 on v4

--- a/solution.py
+++ b/solution.py
@@ -620,9 +620,10 @@
         radial(yf, c, inside)
         joints(yf, c)
         energy(c, inside)
-    for c in range(2):
-        rims_finish(yf, c, 1, y_flights[c])
-        energy(c, outside)
+    rims_finish(yf, 0, 1, y_flights[0])
+    rims_finish(yf, 1, 1, y_flights[1])
+    energy(0, outside)
+    energy(1, outside)
 
     sums = jnp.concatenate(
         [jnp.sum(acc[c, k], axis=0, keepdims=True) for c in range(2) for k in range(4)], axis=0

time: 55.2 us -> 54.5 us (0.987)
  the two profiles are of different devices: /device:TPU:1 before, /device:TPU:2 now
where the time goes in v5:
time: 54.5 us; the launch traced here: 53.5 us
  Pallas kernels  52.9 us (97%)
  between operations  0.64 us (1%)
    pallas_call x1, Pallas kernels, body(): pl.pallas_call(functools.partial(kernel, size_e), out_shape=[pltpu.VMEM((...  51.8 us
    pallas_call x1, Pallas kernels, body(): pl.pallas_call(combine_kernel, out_shape=[jax.ShapeDtypeStruct((rows, LAN...  1.13 us

profile of v5, /device:TPU:2, one launch (start us, length us, event | category | flops | bytes accessed | tf_op | source)
XLA Modules:
  0.0 53.5 jit_solution(16110247596537217888)
XLA Ops:
  0.6 51.8 %shard_map.95 = (f32[1296,128]{1,0:T(8,128)S(1)}, f32[1296,128]{1,0:T(8,128)S(1)}, f32[1296,128]{1,0:T(8,128)S(1)}, f32[1296,128]{1,0:T(8,128)S(1)}, f32[8,128]{1,0:T(8,128)S(1)}) custom-call(f32[1296,128]{1,0:T(8,128)} %bitcast.5, f32[1296,128]{1,0:T(8,128)} %bitcast.6, f32[8,16,81]{2,1,0:T(8,128)} %bitcast.7, s32[16]{0:T(128)} %slots.1, ...), custom_call_target="tpu_custom_call" | custom-call | tf_op jit(solution)/shard_map/pallas_call | solution.py:706
  52.4 1.1 %shard_map.96 = (f32[1296,128]{1,0:T(8,128)}, f32[1296,128]{1,0:T(8,128)}) custom-call(f32[1296,128]{1,0:T(8,128)S(1)} %get-tuple-element.9.b_x, f32[1296,128]{1,0:T(8,128)S(1)} %get-tuple-element.10.b_y, f32[1296,128]{1,0:T(8,128)S(1)} %get-tuple-element.11.y_x, f32[1296,128]{1,0:T(8,128)S(1)} %get-tuple-element.12.y_y, f32[8,128]{1,0:T(8,128)S(1)} %get-tuple-element.13.coef), custom_call_target="tpu_custom_call" | custom-call | tf_op jit(solution)/shard_map/pallas_call | solution.py:765
